TPU v7x, 256 devices: a whole 4x4x8 slice. The times are simulated.
256 devices in a mesh: pt: 8 (over y, core), row: 8 (over z), col: 4 (over x).
Axes of the slice: x: 4, y: 4, z: 8, core: 2. Of those that a mesh axis runs over, the one named last changes fastest.
Arguments:
- jac_cam: float32 [8, 2, 9, 524288], P(None, None, None, ('pt', 'row', 'col')), may hold values from -6 to 6
- jac_pt: float32 [8, 2, 3, 524288], P(None, None, None, ('pt', 'row', 'col')), may hold values from -6 to 6
- obs_cam: int32 [8, 524288], P(None, ('pt', 'row', 'col')), may hold values from 0 to 63
- point_covisible_tile: int32 [524288, 1], P(('pt', 'row', 'col')), may hold values from 0 to 31; in each aligned block of 2048 rows (0 to 2047, 2048 to 4095, ...) at most 128 rows name the same one
Outputs:
- upper_schur_tiles: float32 [32, 576, 576], P(('row', 'col'), 'pt')
- lower_tiles: float32 [32, 576, 576], P(('row', 'col'), 'pt')
Inputs may be any that keep to these rules, and one draw needn't show every extreme that they name: `point_covisible_tile`: among the 2048 points of one device no tile is named by more than 128 points, a bound that some block reaches.
All inputs are finite; a program needn't handle non-finite values.
Results may differ from a plain program's by a relative error of at most 0.0047.
Values sent between devices are 32-bit elements; how exact they have to be, the bound alone decides.
A program may use at most 64 MiB of HBM per device.

v0:
```python
import jax
import jax.numpy as jnp
from jax import lax
from jax.sharding import PartitionSpec as P

CAMB = 64


DAMPING = 1.0


def partner(value, axis, stride):
    mask = 2**stride
    pairs = [(source, source ^ mask) for source in range(lax.axis_size(axis))]
    return lax.ppermute(value, axis, pairs)


def inverse_entries(point_jac):
    normal_matrix = [[None, None, None], [None, None, None], [None, None, None]]
    for first in range(3):
        for second in range(first, 3):
            element = jnp.sum(point_jac[:, :, first, :] * point_jac[:, :, second, :], axis=(0, 1))
            if first == second:
                element = element + DAMPING
            normal_matrix[first][second] = element
            normal_matrix[second][first] = element
    vzz = normal_matrix[0][0]
    vzo = normal_matrix[0][1]
    vzt = normal_matrix[0][2]
    voo = normal_matrix[1][1]
    vot = normal_matrix[1][2]
    vtt = normal_matrix[2][2]
    adj_zz = voo * vtt - vot * vot
    adj_zo = vzt * vot - vzo * vtt
    adj_zt = vzo * vot - vzt * voo
    adj_oo = vzz * vtt - vzt * vzt
    adj_ot = vzo * vzt - vzz * vot
    adj_tt = vzz * voo - vzo * vzo
    determinant = vzz * adj_zz + vzo * adj_zo + vzt * adj_zt
    reciprocal = 1.0 / determinant
    adjugate = [[adj_zz, adj_zo, adj_zt], [adj_zo, adj_oo, adj_ot], [adj_zt, adj_ot, adj_tt]]
    return jnp.stack([jnp.stack(line, 0) for line in adjugate], 0) * reciprocal[None, None, :]


def tile_factors(camera_jac, point_jac, cameras):
    points = camera_jac.shape[-1]
    halfway = camera_jac.shape[0] // 2
    inverse = inverse_entries(point_jac)
    cross_terms = jnp.sum(camera_jac[:, :, :, None, :] * point_jac[:, :, None, :, :], axis=1)
    scaled = jnp.sum(cross_terms[:, :, :, None, :] * inverse[None, None, :, :, :], axis=2)
    labels = jnp.arange(CAMB, dtype=jnp.int32)[:, None, None, None]
    left_factor = jnp.zeros((CAMB, 9, 3, points), jnp.float32)
    right_factor = jnp.zeros((CAMB, 9, 3, points), jnp.float32)
    for obs_index in range(halfway):
        left_factor = left_factor + jnp.where(
            cameras[obs_index][None, None, None, :] == labels, scaled[obs_index][None], 0.0
        )
        right_factor = right_factor + jnp.where(
            cameras[halfway + obs_index][None, None, None, :] == labels,
            cross_terms[halfway + obs_index][None],
            0.0,
        )
    left_factor = left_factor.reshape(CAMB * 9, 3 * points).astype(jnp.bfloat16)
    right_factor = right_factor.reshape(CAMB * 9, 3 * points).astype(jnp.bfloat16)
    return (left_factor, right_factor)


def body(jac_cam, jac_pt, obs_cam, point_covisible_tile):
    groups = lax.axis_size(("row", "col"))
    observed = jac_cam.shape[0]
    held = jac_cam.shape[-1]
    capacity = 2 * held // groups
    tile_ids = point_covisible_tile[:, 0]
    member = (tile_ids[:, None] == jnp.arange(groups, dtype=jnp.int32)[None, :]).astype(jnp.int32)
    before = jnp.cumsum(member, axis=0) - member
    slot_rank = jnp.sum(before * member, axis=1)
    position = tile_ids * capacity + slot_rank
    floats = jnp.concatenate(
        [jac_cam.reshape(observed * 18, held), jac_pt.reshape(observed * 6, held)], axis=0
    )
    feature_rows = floats.shape[0]
    send_floats = (
        jnp.zeros((feature_rows, groups * capacity), jnp.float32).at[:, position].set(floats)
    )
    send_ints = jnp.zeros((observed, groups * capacity), jnp.int32).at[:, position].set(obs_cam)
    recv_floats, recv_ints = (
        lax.all_to_all(
            send_floats.reshape(feature_rows, groups, capacity),
            ("row", "col"),
            split_axis=1,
            concat_axis=1,
            tiled=True,
        ),
        lax.all_to_all(
            send_ints.reshape(observed, groups, capacity),
            ("row", "col"),
            split_axis=1,
            concat_axis=1,
            tiled=True,
        ),
    )
    slot_count = groups * capacity
    recv_floats = recv_floats.reshape(feature_rows, slot_count)
    recv_ints = recv_ints.reshape(observed, slot_count)
    block_points = min(512, slot_count)
    turn_count = slot_count // block_points
    params_width = 9 * CAMB

    def accumulate(turn_index, partial_value):
        first_point = turn_index * block_points
        block_floats = lax.dynamic_slice_in_dim(recv_floats, first_point, block_points, 1)
        block_ints = lax.dynamic_slice_in_dim(recv_ints, first_point, block_points, 1)
        camera_jac = block_floats[: observed * 18].reshape(observed, 2, 9, block_points)
        point_jac = block_floats[observed * 18 :].reshape(observed, 2, 3, block_points)
        left_factor, right_factor = tile_factors(camera_jac, point_jac, block_ints)
        product = lax.dot_general(
            left_factor, right_factor, (((1,), (1,)), ((), ())), preferred_element_type=jnp.float32
        )
        return partial_value - product

    partial_value = lax.fori_loop(
        0, turn_count, accumulate, jnp.zeros((params_width, params_width), jnp.float32)
    )
    upper_share, columns = (
        lax.psum_scatter(partial_value, "pt", scatter_dimension=0, tiled=True),
        lax.psum_scatter(partial_value, "pt", scatter_dimension=1, tiled=True),
    )
    flipped = columns.T
    lower_share = partner(flipped, ("row", "col"), groups.bit_length() - 2)
    return (upper_share[None], lower_share[None])


def solution(mesh):
    in_specs = (
        P(None, None, None, ("pt", "row", "col")),
        P(None, None, None, ("pt", "row", "col")),
        P(None, ("pt", "row", "col")),
        P(("pt", "row", "col"), None),
    )
    out_specs = (P(("row", "col"), "pt", None), P(("row", "col"), "pt", None))
    return jax.shard_map(body, mesh=mesh, in_specs=in_specs, out_specs=out_specs, check_vma=False)
```

profile of v0, /device:TPU:1, one launch (start us, length us, event | category | flops | bytes accessed | tf_op | source)
XLA Modules:
  0.0 380.5 jit_solution(1352312593303886305)
XLA Ops:
  8.0 9.1 %reduce-window.6 = s32[32,16,128]{2,1,0:T(8,128)S(1)} reduce-window(s32[32,16,128]{2,1,0:T(8,128)S(1)} %fusion.7, s32[]{:T(128)} %constant.51.clone.1), window={size=1x1x128 pad=0_0x0_0x127_0}, to_apply=%region_0.0 | reduce-window | flops 8323072 | bytes 524292 | tf_op jit(solution)/shard_map/reduce-window
  22.4 11.6 %scatter_custom_fusion.1 = f32[192,4096]{0,1:T(8,128)} fusion(s32[2048]{0:T(1024)S(1)} %bitcast.162, f32[2048,192]{1,0:T(8,128)} %copy.46, f32[]{:T(128)} %constant.52.clone.1), kind=kCustom, calls=%fused_computation.43 | custom fusion | bytes 3146240 | tf_op jit(solution)/shard_map/scatter | solution.py:83
  34.0 5.3 %copy.47 = f32[192,32,128]{2,0,1:T(8,128)} copy(f32[192,32,128]{0,2,1:T(8,128)} %bitcast.137) | data formatting | bytes 6291456 | tf_op jit(solution)/shard_map/reshape | solution.py:88
  39.3 12.0 %all-to-all-start.1 = ((f32[192,32,128]{2,0,1:T(8,128)}), f32[192,32,128]{2,0,1:T(8,128)S(1)}, u32[]{:S(2)}, u32[]{:S(2)}) async-start(f32[192,32,128]{2,0,1:T(8,128)} %copy.47), calls=%async_computation.1 | async-start | bytes 6291456 | tf_op jit(solution)/shard_map/all_to_all | solution.py:87
  52.6 7.4 %scatter_custom_fusion = s32[8,4096]{0,1:T(8,128)} fusion(s32[2048]{0:T(1024)S(1)} %bitcast.163, s32[2048,8]{1,0:T(8,128)} %copy.42, s32[]{:T(128)} %constant.51.clone.1), kind=kCustom, calls=%fused_computation.46 | custom fusion | bytes 131584 | tf_op jit(solution)/shard_map/scatter | solution.py:85
  62.8 58.8 %all-to-all-done.1 = f32[192,32,128]{2,0,1:T(8,128)S(1)} async-done(((f32[192,32,128]{2,0,1:T(8,128)}), f32[192,32,128]{2,0,1:T(8,128)S(1)}, u32[]{:S(2)}, u32[]{:S(2)}) %all-to-all-start.1) | async-done | bytes 3145760 | tf_op jit(solution)/shard_map/all_to_all | solution.py:87
  121.6 7.9 %all-to-all-start = ((s32[8,32,128]{2,0,1:T(8,128)}), s32[8,32,128]{2,0,1:T(8,128)S(1)}, u32[]{:S(2)}, u32[]{:S(2)}) async-start(s32[8,32,128]{2,0,1:T(8,128)} %copy.43), calls=%async_computation | async-start | bytes 262144 | tf_op jit(solution)/shard_map/all_to_all | solution.py:94
  131.8 7.1 %all-to-all-done = s32[8,32,128]{2,0,1:T(8,128)S(1)} async-done(((s32[8,32,128]{2,0,1:T(8,128)}), s32[8,32,128]{2,0,1:T(8,128)S(1)}, u32[]{:S(2)}, u32[]{:S(2)}) %all-to-all-start) | async-done | bytes 131104 | tf_op jit(solution)/shard_map/all_to_all | solution.py:94
  138.9 164.2 %while.14 = (s32[]{:T(128)}, f32[576,576]{1,0:T(8,128)}, s32[8,4096]{1,0:T(8,128)S(1)}, f32[192,4096]{1,0:T(8,128)}, s32[]{:T(128)}, /*index=5*/s32[]{:T(128)}, ...) while((s32[]{:T(128)}, f32[576,576]{1,0:T(8,128)}, ...), condition=%wide.region_14.15_spmd.clone, body=%wide.region_5.14_spmd.clone.sunk | while | flops 1035314176 | bytes 23900500 | solution.py:121
  141.7 4.9 %add_convert_fusion.5 = bf16[64,9,3,512]{3,2,1,0:T(4,128)(2,1)S(1)} fusion(f32[9,3,512]{2,1,0:T(4,128)S(1)} %get-tuple-element.260, f32[9,3,512]{2,1,0:T(4,128)S(1)} %get-tuple-element.261, f32[9,3,512]{2,1,0:T(4,128)S(1)} %get-tuple-element.264, f32[9,3,512]{2,1,0:T(4,128)S(1)} %get-tuple-element.265, pred[64,512]{1,0:T(8,128)(4,1)S(1)} %get-tuple-element.268, ...), kind=kLoop, calls=%fused_computation.2.clone.1 | loop fusion | flops 7077888 | bytes 2121728 | tf_op jit(solution)/shard_map/while/body/eval_jaxpr/convert_element_type | solution.py:64
  161.8 4.9 %add_convert_fusion.5 = bf16[64,9,3,512]{3,2,1,0:T(4,128)(2,1)S(1)} fusion(f32[9,3,512]{2,1,0:T(4,128)S(1)} %get-tuple-element.260, f32[9,3,512]{2,1,0:T(4,128)S(1)} %get-tuple-element.261, f32[9,3,512]{2,1,0:T(4,128)S(1)} %get-tuple-element.264, f32[9,3,512]{2,1,0:T(4,128)S(1)} %get-tuple-element.265, pred[64,512]{1,0:T(8,128)(4,1)S(1)} %get-tuple-element.268, ...), kind=kLoop, calls=%fused_computation.2.clone.1 | loop fusion | flops 7077888 | bytes 2121728 | tf_op jit(solution)/shard_map/while/body/eval_jaxpr/convert_element_type | solution.py:64
  182.4 4.9 %add_convert_fusion.5 = bf16[64,9,3,512]{3,2,1,0:T(4,128)(2,1)S(1)} fusion(f32[9,3,512]{2,1,0:T(4,128)S(1)} %get-tuple-element.260, f32[9,3,512]{2,1,0:T(4,128)S(1)} %get-tuple-element.261, f32[9,3,512]{2,1,0:T(4,128)S(1)} %get-tuple-element.264, f32[9,3,512]{2,1,0:T(4,128)S(1)} %get-tuple-element.265, pred[64,512]{1,0:T(8,128)(4,1)S(1)} %get-tuple-element.268, ...), kind=kLoop, calls=%fused_computation.2.clone.1 | loop fusion | flops 7077888 | bytes 2121728 | tf_op jit(solution)/shard_map/while/body/eval_jaxpr/convert_element_type | solution.py:64
  188.8 4.9 %add_convert_fusion.4 = bf16[64,9,3,512]{3,2,1,0:T(4,128)(2,1)S(1)} fusion(f32[9,3,512]{2,1,0:T(4,128)S(1)} %get-tuple-element.244, f32[9,3,512]{2,1,0:T(4,128)S(1)} %get-tuple-element.245, f32[9,3,512]{2,1,0:T(4,128)S(1)} %get-tuple-element.248, f32[9,3,512]{2,1,0:T(4,128)S(1)} %get-tuple-element.249, pred[64,512]{1,0:T(8,128)(4,1)S(1)} %get-tuple-element.252, ...), kind=kLoop, calls=%fused_computation.3.clone.1 | loop fusion | flops 7077888 | bytes 2121728 | tf_op jit(solution)/shard_map/while/body/eval_jaxpr/convert_element_type | solution.py:63
  203.0 4.9 %add_convert_fusion.5 = bf16[64,9,3,512]{3,2,1,0:T(4,128)(2,1)S(1)} fusion(f32[9,3,512]{2,1,0:T(4,128)S(1)} %get-tuple-element.260, f32[9,3,512]{2,1,0:T(4,128)S(1)} %get-tuple-element.261, f32[9,3,512]{2,1,0:T(4,128)S(1)} %get-tuple-element.264, f32[9,3,512]{2,1,0:T(4,128)S(1)} %get-tuple-element.265, pred[64,512]{1,0:T(8,128)(4,1)S(1)} %get-tuple-element.268, ...), kind=kLoop, calls=%fused_computation.2.clone.1 | loop fusion | flops 7077888 | bytes 2121728 | tf_op jit(solution)/shard_map/while/body/eval_jaxpr/convert_element_type | solution.py:64
  209.3 4.9 %add_convert_fusion.4 = bf16[64,9,3,512]{3,2,1,0:T(4,128)(2,1)S(1)} fusion(f32[9,3,512]{2,1,0:T(4,128)S(1)} %get-tuple-element.244, f32[9,3,512]{2,1,0:T(4,128)S(1)} %get-tuple-element.245, f32[9,3,512]{2,1,0:T(4,128)S(1)} %get-tuple-element.248, f32[9,3,512]{2,1,0:T(4,128)S(1)} %get-tuple-element.249, pred[64,512]{1,0:T(8,128)(4,1)S(1)} %get-tuple-element.252, ...), kind=kLoop, calls=%fused_computation.3.clone.1 | loop fusion | flops 7077888 | bytes 2121728 | tf_op jit(solution)/shard_map/while/body/eval_jaxpr/convert_element_type | solution.py:63
  223.6 4.9 %add_convert_fusion.5 = bf16[64,9,3,512]{3,2,1,0:T(4,128)(2,1)S(1)} fusion(f32[9,3,512]{2,1,0:T(4,128)S(1)} %get-tuple-element.260, f32[9,3,512]{2,1,0:T(4,128)S(1)} %get-tuple-element.261, f32[9,3,512]{2,1,0:T(4,128)S(1)} %get-tuple-element.264, f32[9,3,512]{2,1,0:T(4,128)S(1)} %get-tuple-element.265, pred[64,512]{1,0:T(8,128)(4,1)S(1)} %get-tuple-element.268, ...), kind=kLoop, calls=%fused_computation.2.clone.1 | loop fusion | flops 7077888 | bytes 2121728 | tf_op jit(solution)/shard_map/while/body/eval_jaxpr/convert_element_type | solution.py:64
  229.9 4.9 %add_convert_fusion.4 = bf16[64,9,3,512]{3,2,1,0:T(4,128)(2,1)S(1)} fusion(f32[9,3,512]{2,1,0:T(4,128)S(1)} %get-tuple-element.244, f32[9,3,512]{2,1,0:T(4,128)S(1)} %get-tuple-element.245, f32[9,3,512]{2,1,0:T(4,128)S(1)} %get-tuple-element.248, f32[9,3,512]{2,1,0:T(4,128)S(1)} %get-tuple-element.249, pred[64,512]{1,0:T(8,128)(4,1)S(1)} %get-tuple-element.252, ...), kind=kLoop, calls=%fused_computation.3.clone.1 | loop fusion | flops 7077888 | bytes 2121728 | tf_op jit(solution)/shard_map/while/body/eval_jaxpr/convert_element_type | solution.py:63
  244.2 4.9 %add_convert_fusion.5 = bf16[64,9,3,512]{3,2,1,0:T(4,128)(2,1)S(1)} fusion(f32[9,3,512]{2,1,0:T(4,128)S(1)} %get-tuple-element.260, f32[9,3,512]{2,1,0:T(4,128)S(1)} %get-tuple-element.261, f32[9,3,512]{2,1,0:T(4,128)S(1)} %get-tuple-element.264, f32[9,3,512]{2,1,0:T(4,128)S(1)} %get-tuple-element.265, pred[64,512]{1,0:T(8,128)(4,1)S(1)} %get-tuple-element.268, ...), kind=kLoop, calls=%fused_computation.2.clone.1 | loop fusion | flops 7077888 | bytes 2121728 | tf_op jit(solution)/shard_map/while/body/eval_jaxpr/convert_element_type | solution.py:64
  250.5 4.9 %add_convert_fusion.4 = bf16[64,9,3,512]{3,2,1,0:T(4,128)(2,1)S(1)} fusion(f32[9,3,512]{2,1,0:T(4,128)S(1)} %get-tuple-element.244, f32[9,3,512]{2,1,0:T(4,128)S(1)} %get-tuple-element.245, f32[9,3,512]{2,1,0:T(4,128)S(1)} %get-tuple-element.248, f32[9,3,512]{2,1,0:T(4,128)S(1)} %get-tuple-element.249, pred[64,512]{1,0:T(8,128)(4,1)S(1)} %get-tuple-element.252, ...), kind=kLoop, calls=%fused_computation.3.clone.1 | loop fusion | flops 7077888 | bytes 2121728 | tf_op jit(solution)/shard_map/while/body/eval_jaxpr/convert_element_type | solution.py:63
  264.8 4.9 %add_convert_fusion.5 = bf16[64,9,3,512]{3,2,1,0:T(4,128)(2,1)S(1)} fusion(f32[9,3,512]{2,1,0:T(4,128)S(1)} %get-tuple-element.260, f32[9,3,512]{2,1,0:T(4,128)S(1)} %get-tuple-element.261, f32[9,3,512]{2,1,0:T(4,128)S(1)} %get-tuple-element.264, f32[9,3,512]{2,1,0:T(4,128)S(1)} %get-tuple-element.265, pred[64,512]{1,0:T(8,128)(4,1)S(1)} %get-tuple-element.268, ...), kind=kLoop, calls=%fused_computation.2.clone.1 | loop fusion | flops 7077888 | bytes 2121728 | tf_op jit(solution)/shard_map/while/body/eval_jaxpr/convert_element_type | solution.py:64
  285.3 4.9 %add_convert_fusion.5 = bf16[64,9,3,512]{3,2,1,0:T(4,128)(2,1)S(1)} fusion(f32[9,3,512]{2,1,0:T(4,128)S(1)} %get-tuple-element.260, f32[9,3,512]{2,1,0:T(4,128)S(1)} %get-tuple-element.261, f32[9,3,512]{2,1,0:T(4,128)S(1)} %get-tuple-element.264, f32[9,3,512]{2,1,0:T(4,128)S(1)} %get-tuple-element.265, pred[64,512]{1,0:T(8,128)(4,1)S(1)} %get-tuple-element.268, ...), kind=kLoop, calls=%fused_computation.2.clone.1 | loop fusion | flops 7077888 | bytes 2121728 | tf_op jit(solution)/shard_map/while/body/eval_jaxpr/convert_element_type | solution.py:64
  306.9 29.0 %reduce-scatter.9.cloned.1.call-done = f32[576,72]{0,1:T(8,128)} async-done(((f32[576,576]{0,1:T(8,128)}), f32[576,72]{0,1:T(8,128)}) %reduce-scatter.9.cloned.1.call-update) | async-done | bytes 165904
  335.9 5.2 %collective-permute-start = (f32[72,576]{1,0:T(8,128)}, f32[72,576]{1,0:T(8,128)S(1)}, u32[]{:S(2)}, u32[]{:S(2)}) collective-permute-start(f32[72,576]{1,0:T(8,128)} %bitcast.165), channel_id=1, source_target_pairs={{0,16},{1,17},{2,18},{3,19},{4,20},{5,21},{6,22},{7,23},{8,24},{9,... | collective-permute-start | bytes 497672 | tf_op jit(solution)/shard_map/ppermute | solution.py:15
  344.5 28.5 %reduce-scatter.7.cloned.1.call-done = f32[72,576]{1,0:T(8,128)} async-done(((f32[576,576]{1,0:T(8,128)}), f32[72,576]{1,0:T(8,128)}) %reduce-scatter.7.cloned.1.call-update) | async-done | bytes 165904
  (242 shorter events, 123.8 us)
Async XLA Ops:
  7.2 10.6 %copy-start.1 = (s32[2048,1]{0,1:T(1,128)S(1)}, s32[2048,1]{0,1:T(1,128)}, u32[]{:S(2)}) copy-start(s32[2048,1]{0,1:T(1,128)} %param.9) | copy-start | bytes 24580
  7.2 10.8 %copy-start = (f32[8,2,9,2048]{3,1,2,0:T(2,128)S(1)}, f32[8,2,9,2048]{3,1,2,0:T(2,128)}, u32[]{:S(2)}) copy-start(f32[8,2,9,2048]{3,1,2,0:T(2,128)} %param.6) | copy-start | bytes 3538948
  39.3 12.0 %copy-start.2 = (s32[8,2048]{1,0:T(8,128)S(1)}, s32[8,2048]{1,0:T(8,128)}, u32[]{:S(2)}) copy-start(s32[8,2048]{1,0:T(8,128)} %param.8) | copy-start | bytes 196612
  39.3 82.3 %all-to-all-start.1 = ((f32[192,32,128]{2,0,1:T(8,128)}), f32[192,32,128]{2,0,1:T(8,128)S(1)}, u32[]{:S(2)}, u32[]{:S(2)}) async-start(f32[192,32,128]{2,0,1:T(8,128)} %copy.47), calls=%async_computation.1 | async-start | bytes 6291456 | tf_op jit(solution)/shard_map/all_to_all | solution.py:87
  121.6 17.3 %all-to-all-start = ((s32[8,32,128]{2,0,1:T(8,128)}), s32[8,32,128]{2,0,1:T(8,128)S(1)}, u32[]{:S(2)}, u32[]{:S(2)}) async-start(s32[8,32,128]{2,0,1:T(8,128)} %copy.43), calls=%async_computation | async-start | bytes 262144 | tf_op jit(solution)/shard_map/all_to_all | solution.py:94
  129.5 206.3 %reduce-scatter.9.cloned.1.call-start = ((), (), s32[]{:S(2)}) async-start(), calls=%async_computation.5 | async-start | bytes 1658880
  306.1 66.9 %reduce-scatter.7.cloned.1.call-start = ((), (), s32[]{:S(2)}) async-start(), calls=%async_computation.4 | async-start | bytes 1658880
  335.9 8.6 %collective-permute-start = (f32[72,576]{1,0:T(8,128)}, f32[72,576]{1,0:T(8,128)S(1)}, u32[]{:S(2)}, u32[]{:S(2)}) collective-permute-start(f32[72,576]{1,0:T(8,128)} %bitcast.165), channel_id=1, source_target_pairs={{0,16},{1,17},{2,18},{3,19},{4,20},{5,21},{6,22},{7,23},{8,24},{9,... | collective-permute-start | bytes 497672 | tf_op jit(solution)/shard_map/ppermute | solution.py:15
Sparse Core Ops, SparseCore 0:
  306.2 29.5 reduce-scatter.8
  339.0 33.9 reduce-scatter.6
where the time goes:
time: 383 us; the launch traced here: 381 us
  waiting for transfers between devices  128 us (33%)
  other arithmetic  94.6 us (25%)
  local copies, waits for them, and re-layouts  80.6 us (21%)
  matrix products  36.9 us (10%)
  starting transfers between devices  25.3 us (7%)
  between operations  14.2 us (4%)
    all_to_all x1, waiting for transfers between devices, body(): lax.all_to_all(send_floats.reshape(feature_rows, groups, capacity), ('row...  58.8 us
    unnamed x4, waiting for transfers between devices  58.2 us
    convert_element_type x8, other arithmetic, tile_factors(): right_factor.reshape(CAMB * 9, 3 * points).astype(jnp.bfloat16)  39.6 us
    convert_element_type x8, other arithmetic, tile_factors(): left_factor = left_factor.reshape(CAMB * 9, 3 * points).astype(jnp.bfloat16)  39.5 us
    dot_general x8, matrix products, accumulate(): lax.dot_general(left_factor, right_factor, (((1,), (1,)), ((), ())), pref...  36.9 us
    while x48, local copies, waits for them, and re-layouts  20.6 us
    all_to_all x1, starting transfers between devices, body(): lax.all_to_all(send_floats.reshape(feature_rows, groups, capacity), ('row...  12 us
    scatter x1, local copies, waits for them, and re-layouts, body(): jnp.zeros((feature_rows, groups * capacity), jnp.float32).at[:, position]  11.6 us
  transfers between devices with their start and end apart: 5, of which 5 were waited for; matrix products, arithmetic and copies ran while one was open for 4% of the time, Pallas kernels for 0%

commit v1 on v0

v1 whole, which is shorter than its diff:
```python
import functools

import jax
import jax.numpy as jnp
from jax import lax
from jax.experimental import pallas as pl
from jax.experimental.pallas import tpu as pltpu
from jax.sharding import PartitionSpec as P

F32 = jnp.float32
BF16 = jnp.bfloat16
MESH = pl.DeviceIdType.MESH

CAMB = 64
DAMPING = 1.0
LANES = 128
TILES = 32
FEATURES = 200
PT_ROW = 144
CAM_ROW = 192
GROUP = 4
WIDTH = 9 * CAMB
NT = (((1,), (1,)), ((), ()))
SPLIT = (0, 5, 9)


def point_factors(pt_ref, out_ref):
    def entry(obs, coordinate, residual):
        return pt_ref[pl.ds((obs * 3 + coordinate) * 32 + residual, 16, stride=2), :]

    sums = {}
    for first in range(3):
        for second in range(first, 3):
            total = None
            for obs in range(8):
                for residual in range(2):
                    term = entry(obs, first, residual) * entry(obs, second, residual)
                    total = term if total is None else total + term
            sums[first, second] = total + DAMPING if first == second else total
    vzz, vzo, vzt = sums[0, 0], sums[0, 1], sums[0, 2]
    voo, vot, vtt = sums[1, 1], sums[1, 2], sums[2, 2]
    adj_zz = voo * vtt - vot * vot
    adj_zo = vzt * vot - vzo * vtt
    adj_zt = vzo * vot - vzt * voo
    adj_oo = vzz * vtt - vzt * vzt
    adj_ot = vzo * vzt - vzz * vot
    adj_tt = vzz * voo - vzo * vzo
    reciprocal = 1.0 / (vzz * adj_zz + vzo * adj_zo + vzt * adj_zt)
    inverse = [
        [entry_ * reciprocal for entry_ in line]
        for line in ((adj_zz, adj_zo, adj_zt), (adj_zo, adj_oo, adj_ot), (adj_zt, adj_ot, adj_tt))
    ]
    for residual in range(2):
        for obs in range(8):
            parts = [entry(obs, coordinate, residual) for coordinate in range(3)]
            for coordinate in range(3):
                if obs < 4:
                    value = (
                        parts[0] * inverse[0][coordinate]
                        + parts[1] * inverse[1][coordinate]
                        + parts[2] * inverse[2][coordinate]
                    )
                else:
                    value = parts[coordinate]
                row = (residual * 24 + obs * 3 + coordinate) * 16
                out_ref[row : row + 16, :] = value


def ranks(tile_ref, member_ref, rank_ref):
    for block in range(16):
        ids = jnp.broadcast_to(tile_ref[block : block + 1, :], (TILES, LANES))
        same = ids == lax.broadcasted_iota(jnp.int32, (TILES, LANES), 0)
        member_ref[block * TILES : (block + 1) * TILES, :] = jnp.where(same, 1.0, 0.0).astype(BF16)
    rows = lax.broadcasted_iota(jnp.int32, (LANES, LANES), 0)
    columns = lax.broadcasted_iota(jnp.int32, (LANES, LANES), 1)
    earlier = jnp.where(rows < columns, 1.0, 0.0).astype(BF16)
    members = member_ref[...]
    before = jnp.dot(members, earlier, preferred_element_type=F32)
    totals = jnp.dot(members, jnp.ones((LANES, LANES), BF16), preferred_element_type=F32)
    base = jnp.zeros((TILES, LANES), F32)
    for block in range(16):
        span = slice(block * TILES, (block + 1) * TILES)
        own = members[span].astype(F32) * (before[span] + base)
        rank_ref[block : block + 1, :] = jnp.sum(own, axis=0, keepdims=True)
        base = base + totals[span]


def gather_features(cam_ref, factor_ref, obs_ref, x_ref):
    for block in range(16):
        lanes = slice(block * LANES, (block + 1) * LANES)
        parts = [cam_ref[pl.ds(block * 2 + residual, 72, stride=32), :] for residual in range(2)]
        parts.append(factor_ref[pl.ds(block, 48, stride=16), :])
        values = jnp.concatenate(parts, axis=0)
        high = values.astype(BF16)
        x_ref[0:192, lanes] = high
        x_ref[208:400, lanes] = (values - high.astype(F32)).astype(BF16)
        names = obs_ref[:, lanes].astype(F32) + 1.0
        x_ref[192:208, lanes] = jnp.concatenate([names, jnp.zeros((8, LANES), F32)], axis=0).astype(BF16)


def place_points(x_ref, tile_ref, rank_ref, place_ref, wanted):
    slots = lax.broadcasted_iota(jnp.int32, (LANES, LANES), 0).astype(F32).astype(BF16)
    one, zero = jnp.ones((LANES, LANES), BF16), jnp.zeros((LANES, LANES), BF16)
    for part in range(2):
        slot_of = jnp.where(tile_ref[...] == wanted[part], rank_ref[...], -1.0)
        for block in range(16):
            row = jnp.broadcast_to(slot_of[block : block + 1, :], (LANES, LANES)).astype(BF16)
            place_ref[part * LANES : (part + 1) * LANES, block * LANES : (block + 1) * LANES] = jnp.where(
                row == slots, one, zero
            )
    placed = lax.dot_general(x_ref[...], place_ref[...], NT, preferred_element_type=F32)
    return placed[0:192] + placed[208:400], placed[192:200]


def fill_factor(block_ref, half, factor_ref, position):
    labels = (lax.broadcasted_iota(jnp.int32, (CAMB, LANES), 0).astype(F32) + 1.0).astype(BF16)
    cameras, masks, cross = [], [], []
    for index in range(4):
        obs = 4 * half + index
        camera = block_ref[CAM_ROW + obs : CAM_ROW + obs + 1, :]
        cameras.append(camera)
        masks.append(labels == jnp.broadcast_to(camera, (CAMB, LANES)).astype(BF16))
        camera_rows = [block_ref[res * 72 + obs * 9 : res * 72 + obs * 9 + 9, :] for res in range(2)]
        line = []
        for coordinate in range(3):
            rows = [PT_ROW + res * 24 + obs * 3 + coordinate for res in range(2)]
            line.append(
                camera_rows[0] * block_ref[rows[0] : rows[0] + 1, :]
                + camera_rows[1] * block_ref[rows[1] : rows[1] + 1, :]
            )
        cross.append(line)
    for index in range(4):
        for later in range(index + 1, 4):
            same = cameras[index] == cameras[later]
            for coordinate in range(3):
                cross[index][coordinate] = cross[index][coordinate] + jnp.where(same, cross[later][coordinate], 0.0)
    for coordinate in range(3):
        first = (coordinate * GROUP + position) * LANES
        for parameter in range(9):
            value = jnp.zeros((CAMB, LANES), BF16)
            for index in (3, 2, 1, 0):
                row = cross[index][coordinate][parameter : parameter + 1, :]
                value = jnp.where(masks[index], jnp.broadcast_to(row, (CAMB, LANES)).astype(BF16), value)
            factor_ref[parameter * CAMB : (parameter + 1) * CAMB, first : first + LANES] = value


def split_three(value):
    high = value.astype(BF16)
    rest = value - high.astype(F32)
    middle = rest.astype(BF16)
    return high, middle, (rest - middle.astype(F32)).astype(BF16)


def kernel(
    cam_ref, pt_ref, obs_ref, tile_ref, upper_ref, lower_ref,
    x_ref, factor_ref, member_ref, rank_ref, place_ref, sent_ref, held_ref, left_ref, right_ref,
    total_ref, ring_a, ring_b, perm_ref, rows_ref, share_ref, flip_ref, blocks_ref,
    sent_sem, held_sem, ring_sent, ring_held, share_sem, flip_sent, flip_held,
):
    pt, row, col = lax.axis_index("pt"), lax.axis_index("row"), lax.axis_index("col")
    y, core = pt // 2, lax.rem(pt, 2)
    mirror = lax.rem(row + 4, 8)
    same = (pt == row).astype(jnp.int32)
    flip_self = (pt == mirror).astype(jnp.int32)

    def chip_at(pair):
        return lax.rem(y + pair // 4, 4), lax.rem(col + lax.rem(pair, 4), 4)

    def core_at(part):
        return core if part == 0 else 1 - core

    barrier = pltpu.get_barrier_semaphore()

    def greet(pair, _):
        there_y, there_x = chip_at(pair)
        for part in range(2):
            pl.semaphore_signal(
                barrier, inc=1, device_id=(there_y * 2 + core_at(part), row, there_x), device_id_type=MESH
            )
        return 0

    lax.fori_loop(1, 16, greet, 0)
    pl.semaphore_signal(barrier, inc=1, device_id=(y * 2 + 1 - core, row, col), device_id_type=MESH)
    ahead, behind = lax.rem(row + 1, 8), lax.rem(row + 7, 8)
    pl.semaphore_signal(barrier, inc=1, device_id=(pt, ahead, col), device_id_type=MESH)
    pl.semaphore_signal(barrier, inc=1, device_id=(pt, behind, col), device_id_type=MESH)

    @pl.when(same == 0)
    def _():
        pl.semaphore_signal(barrier, inc=1, device_id=(row, pt, col), device_id_type=MESH)

    def greet_flip(other, _):
        @pl.when((pt != mirror) | (row != other))
        def _():
            pl.semaphore_signal(barrier, inc=1, device_id=(mirror, other, col), device_id_type=MESH)

        return 0

    lax.fori_loop(0, 8, greet_flip, 0)

    point_factors(pt_ref, factor_ref)
    ranks(tile_ref, member_ref, rank_ref)
    gather_features(cam_ref, factor_ref, obs_ref, x_ref)

    pl.semaphore_wait(barrier, 31 + 2 + (1 - same) + 8 - flip_self)

    def dispatch(index, there):
        return pltpu.make_async_remote_copy(
            src_ref=sent_ref.at[index],
            dst_ref=held_ref.at[index],
            send_sem=sent_sem.at[index],
            recv_sem=held_sem.at[index],
            device_id=there,
            device_id_type=MESH,
        )

    def send_pair(pair, _):
        there_y, there_x = chip_at(pair)
        owners = [there_y * 2 + core_at(part) for part in range(2)]
        placed, names = place_points(
            x_ref, tile_ref, rank_ref, place_ref, [owner * 4 + there_x for owner in owners]
        )
        for part in range(2):
            lanes = slice(part * LANES, (part + 1) * LANES)
            sent_ref[2 * pair + part, 0:192, :] = placed[:, lanes]
            sent_ref[2 * pair + part, 192:200, :] = names[:, lanes]
            dispatch(2 * pair + part, (owners[part], row, there_x)).start()
        return 0

    lax.fori_loop(1, 16, send_pair, 0)
    sibling = y * 2 + 1 - core
    placed, names = place_points(x_ref, tile_ref, rank_ref, place_ref, [pt * 4 + col, sibling * 4 + col])
    sent_ref[1, 0:192, :] = placed[:, LANES:]
    sent_ref[1, 192:200, :] = names[:, LANES:]
    dispatch(1, (sibling, row, col)).start()
    held_ref[0, 0:192, :] = placed[:, :LANES]
    held_ref[0, 192:200, :] = names[:, :LANES]

    source = lax.broadcasted_iota(jnp.int32, (WIDTH, WIDTH), 1)
    goal = lax.broadcasted_iota(jnp.int32, (WIDTH, WIDTH), 0)
    target = (source & 63) * 9 + (source >> 6)
    perm_ref[...] = jnp.where(target == goal, 1.0, 0.0).astype(BF16)

    total_ref[...] = jnp.zeros_like(total_ref)

    def add_group(group, _):
        for position in range(GROUP):
            index = group * GROUP + position

            @pl.when(index > 0)
            def _():
                dispatch(index, (pt, row, col)).wait_recv()

        for position in range(GROUP):
            block = held_ref.at[group * GROUP + position]
            fill_factor(block, 0, left_ref, position)
            fill_factor(block, 1, right_ref, position)
        product = lax.dot_general(left_ref[...], right_ref[...], NT, preferred_element_type=F32)
        total_ref[...] -= product.reshape(9, CAMB, WIDTH)
        return 0

    lax.fori_loop(0, TILES // GROUP, add_group, 0)

    ways = (jnp.where(core == 0, 1, 7), jnp.where(core == 0, 7, 1))
    rings = (ring_a, ring_b)

    def hop(step, ring):
        first, last = SPLIT[ring], SPLIT[ring + 1]
        if step == 0:
            piece = lax.rem(row + 8 - ways[ring], 8)
            source_ref = total_ref.at[first:last, pl.ds(pl.multiple_of(piece * 8, 8), 8), :]
        else:
            source_ref = rings[ring].at[step - 1]
        return pltpu.make_async_remote_copy(
            src_ref=source_ref,
            dst_ref=rings[ring].at[step],
            send_sem=ring_sent.at[ring, step],
            recv_sem=ring_held.at[ring, step],
            device_id=(pt, lax.rem(row + ways[ring], 8), col),
            device_id_type=MESH,
        )

    for ring in range(2):
        hop(0, ring).start()
    for step in range(7):
        for ring in range(2):
            first, last = SPLIT[ring], SPLIT[ring + 1]
            hop(step, ring).wait_recv()
            piece = lax.rem(row + 8 * (step + 2) - (step + 2) * ways[ring], 8)
            mine = total_ref[first:last, pl.ds(pl.multiple_of(piece * 8, 8), 8), :]
            if step < 6:
                rings[ring][step] = rings[ring][step] + mine
                hop(step + 1, ring).start()
            else:
                for parameter in range(first, last):
                    sums = rings[ring][step, parameter - first] + mine[parameter - first]
                    for camera in range(8):
                        goal_row = camera * 9 + parameter
                        rows_ref[goal_row : goal_row + 1, :] = sums[camera : camera + 1]

    stacked = jnp.concatenate(split_three(rows_ref[...]), axis=0)
    ordered = lax.dot_general(stacked, perm_ref[...], NT, preferred_element_type=F32)
    share = ordered[0:72] + ordered[72:144] + ordered[144:216]

    share_ref[...] = share
    upper_copy = pltpu.make_async_remote_copy(
        src_ref=share_ref,
        dst_ref=upper_ref,
        send_sem=share_sem.at[0],
        recv_sem=share_sem.at[1],
        device_id=(row, pt, col),
        device_id_type=MESH,
    )

    @pl.when(same == 0)
    def _():
        upper_copy.start()

    @pl.when(same == 1)
    def _():
        upper_ref[...] = share_ref[...]

    flipped = share.T
    for other in range(8):
        flip_ref[other] = flipped[other * 72 : (other + 1) * 72, :]

    there = lax.rem(pt + 4, 8)

    def flip(other):
        return pltpu.make_async_remote_copy(
            src_ref=flip_ref.at[other],
            dst_ref=blocks_ref.at[row],
            send_sem=flip_sent.at[other],
            recv_sem=flip_held.at[row],
            device_id=(other, there, col),
            device_id_type=MESH,
        )

    def flip_from(other):
        return pltpu.make_async_remote_copy(
            src_ref=flip_ref.at[other],
            dst_ref=blocks_ref.at[other],
            send_sem=flip_sent.at[other],
            recv_sem=flip_held.at[other],
            device_id=(pt, row, col),
            device_id_type=MESH,
        )

    def send_flip(other, _):
        is_self = (other == pt) & (there == row)

        @pl.when(jnp.logical_not(is_self))
        def _():
            flip(other).start()

        @pl.when(is_self)
        def _():
            blocks_ref[row] = flip_ref[other]

        return 0

    lax.fori_loop(0, 8, send_flip, 0)

    for other in range(8):
        @pl.when((mirror != pt) | (row != other))
        def _():
            flip_from(other).wait_recv()

        lower_ref[:, other * 72 : (other + 1) * 72] = blocks_ref[other]

    @pl.when(same == 0)
    def _():
        upper_copy.wait()

    def drain(index, _):
        dispatch(index, (pt, row, col)).wait_send()
        return 0

    lax.fori_loop(1, TILES, drain, 0)
    for step in range(7):
        for ring in range(2):
            hop(step, ring).wait_send()

    def drain_flip(other, _):
        @pl.when((other != pt) | (there != row))
        def _():
            flip(other).wait_send()

        return 0

    lax.fori_loop(0, 8, drain_flip, 0)


def body(jac_cam, jac_pt, obs_cam, point_covisible_tile):
    def rows_of(array):
        observed, _, width, held = array.shape
        array = array.transpose(0, 2, 1, 3).reshape(observed * width, 2, held // LANES, LANES)
        return array.transpose(0, 2, 1, 3).reshape(observed * width * 2 * held // LANES, LANES)

    vmem = pl.BlockSpec(memory_space=pltpu.VMEM)
    upper, lower = pl.pallas_call(
        kernel,
        out_shape=[jax.ShapeDtypeStruct((72, WIDTH), F32)] * 2,
        in_specs=[vmem] * 4,
        out_specs=[vmem] * 2,
        scratch_shapes=[
            pltpu.VMEM((400, 2048), BF16),
            pltpu.VMEM((768, LANES), F32),
            pltpu.VMEM((512, LANES), BF16),
            pltpu.VMEM((16, LANES), F32),
            pltpu.VMEM((256, 2048), BF16),
            pltpu.VMEM((TILES, FEATURES, LANES), F32),
            pltpu.VMEM((TILES, FEATURES, LANES), F32),
            pltpu.VMEM((WIDTH, 3 * LANES * GROUP), BF16),
            pltpu.VMEM((WIDTH, 3 * LANES * GROUP), BF16),
            pltpu.VMEM((9, CAMB, WIDTH), F32),
            pltpu.VMEM((7, 5, 8, WIDTH), F32),
            pltpu.VMEM((7, 4, 8, WIDTH), F32),
            pltpu.VMEM((WIDTH, WIDTH), BF16),
            pltpu.VMEM((72, WIDTH), F32),
            pltpu.VMEM((72, WIDTH), F32),
            pltpu.VMEM((8, 72, 72), F32),
            pltpu.VMEM((8, 72, 72), F32),
            pltpu.SemaphoreType.DMA((TILES,)),
            pltpu.SemaphoreType.DMA((TILES,)),
            pltpu.SemaphoreType.DMA((2, 7)),
            pltpu.SemaphoreType.DMA((2, 7)),
            pltpu.SemaphoreType.DMA((2,)),
            pltpu.SemaphoreType.DMA((8,)),
            pltpu.SemaphoreType.DMA((8,)),
        ],
        compiler_params=pltpu.CompilerParams(
            collective_id=0, has_side_effects=True, vmem_limit_bytes=50 * 2**20
        ),
    )(rows_of(jac_cam), rows_of(jac_pt), obs_cam, point_covisible_tile.reshape(16, LANES))
    return (upper[None], lower[None])


def solution(mesh):
    in_specs = (
        P(None, None, None, ("pt", "row", "col")),
        P(None, None, None, ("pt", "row", "col")),
        P(None, ("pt", "row", "col")),
        P(("pt", "row", "col"), None),
    )
    out_specs = (P(("row", "col"), "pt", None), P(("row", "col"), "pt", None))
    return jax.shard_map(body, mesh=mesh, in_specs=in_specs, out_specs=out_specs, check_vma=False)
```

time: 383 us -> 124 us (0.32)
  waiting for transfers between devices: 128 us -> 0 us
  Pallas kernels: 0 us -> 116 us
  other arithmetic: 94.6 us -> 0 us
  local copies, waits for them, and re-layouts: 80.6 us -> 5.14 us
  matrix products: 36.9 us -> 0 us
  starting transfers between devices: 25.3 us -> 0 us
  between operations: 14.2 us -> 0.65 us
    pallas_call x0 -> x1, Pallas kernels: none -> 116 us  [body(): pl.pallas_call(kernel, out_shape=[jax.ShapeDtypeStruct((72, WIDTH), F32)]...]
    convert_element_type x17 -> x0, other arithmetic: 79.9 us -> none  [the longest x8 39.6 us: tile_factors(): right_factor.reshape(CAMB * 9, 3 * points).astype(jnp.bfloat16)]
    all_to_all x2 -> x0, waiting for transfers between devices: 65.9 us -> none  [the longest x1 58.8 us: body(): lax.all_to_all(send_floats.reshape(feature_rows, groups, capacity), ('row...]
    unnamed x4 -> x0, waiting for transfers between devices: 58.2 us -> none
    dot_general x8 -> x0, matrix products: 36.9 us -> none  [accumulate(): lax.dot_general(left_factor, right_factor, (((1,), (1,)), ((), ())), pref...]
    while x49 -> x0, local copies, waits for them, and re-layouts: 23.6 us -> none
    all_to_all x2 -> x0, starting transfers between devices: 19.9 us -> none  [the longest x1 12 us: body(): lax.all_to_all(send_floats.reshape(feature_rows, groups, capacity), ('row...]
    scatter x2 -> x0, local copies, waits for them, and re-layouts: 19 us -> none  [the longest x1 11.6 us: body(): jnp.zeros((feature_rows, groups * capacity), jnp.float32).at[:, position]]
  transfers between devices with their start and end apart: 5 -> 0, of which waited for: 5 -> 0; matrix products, arithmetic and copies ran while one was open for 4% -> 0% of each run, Pallas kernels for 0% -> 0%
where the time goes in v1:
time: 124 us; the launch traced here: 121 us
  Pallas kernels  116 us (94%)
  local copies, waits for them, and re-layouts  5.14 us (4%)
    pallas_call x1, Pallas kernels, body(): pl.pallas_call(kernel, out_shape=[jax.ShapeDtypeStruct((72, WIDTH), F32)]...  116 us
    unnamed x10, local copies, waits for them, and re-layouts  5.14 us

profile of v1, /device:TPU:1, one launch (start us, length us, event | category | flops | bytes accessed | tf_op | source)
XLA Modules:
  0.0 121.4 jit_solution(12579126866801931349)
XLA Ops:
  0.6 0.0 copy-start
  0.6 1.3 %copy-done = f32[8,2,9,2048]{3,1,2,0:T(2,128)S(1)} copy-done((f32[8,2,9,2048]{3,1,2,0:T(2,128)S(1)}, f32[8,2,9,2048]{3,1,2,0:T(2,128)}, u32[]{:S(2)}) %copy-start) | copy-done | bytes 1179672
  1.9 0.0 copy-start.1
  1.9 1.0 copy-done.1
  2.9 0.0 copy-start.2
  2.9 0.8 copy-done.2
  3.7 0.0 copy-start.3
  3.7 0.7 copy-done.3
  4.4 115.7 %shard_map.59 = (f32[72,576]{1,0:T(8,128)S(1)}, f32[72,576]{1,0:T(8,128)S(1)}) custom-call(f32[2304,128]{1,0:T(8,128)S(1)} %bitcast.17, f32[768,128]{1,0:T(8,128)S(1)} %bitcast.18, s32[8,2048]{1,0:T(8,128)S(1)} %copy-done.2, s32[16,128]{1,0:T(8,128)S(1)} %bitcast.21), custom_call_target="tpu_custom_call" | custom-call | tf_op jit(solution)/shard_map/pallas_call | solution.py:401
  120.1 0.7 copy.10
  120.8 0.7 copy.11
Async XLA Ops:
  0.6 1.3 %copy-start = (f32[8,2,9,2048]{3,1,2,0:T(2,128)S(1)}, f32[8,2,9,2048]{3,1,2,0:T(2,128)}, u32[]{:S(2)}) copy-start(f32[8,2,9,2048]{3,1,2,0:T(2,128)} %param.4) | copy-start | bytes 3538948
  1.9 1.0 copy-start.1
  2.9 0.8 copy-start.2
  3.7 0.7 copy-start.3

commit v2 on v1

v2 whole, which is shorter than its diff:
```python
import functools

import jax
import jax.numpy as jnp
from jax import lax
from jax.experimental import pallas as pl
from jax.experimental.pallas import tpu as pltpu
from jax.sharding import PartitionSpec as P

F32 = jnp.float32
BF16 = jnp.bfloat16
MESH = pl.DeviceIdType.MESH

CAMB = 64
DAMPING = 1.0
LANES = 128
TILES = 32
FEATURES = 200
PT_ROW = 144
CAM_ROW = 192
GROUP = 4
WIDTH = 9 * CAMB
NT = (((1,), (1,)), ((), ()))
CHUNKS = 3
ROWS = 72 // CHUNKS
TWO_HOP = 7


def point_factors(pt_ref, out_ref):
    def entry(obs, coordinate, residual):
        return pt_ref[pl.ds((obs * 3 + coordinate) * 32 + residual, 16, stride=2), :]

    sums = {}
    for first in range(3):
        for second in range(first, 3):
            total = None
            for obs in range(8):
                for residual in range(2):
                    term = entry(obs, first, residual) * entry(obs, second, residual)
                    total = term if total is None else total + term
            sums[first, second] = total + DAMPING if first == second else total
    vzz, vzo, vzt = sums[0, 0], sums[0, 1], sums[0, 2]
    voo, vot, vtt = sums[1, 1], sums[1, 2], sums[2, 2]
    adj_zz = voo * vtt - vot * vot
    adj_zo = vzt * vot - vzo * vtt
    adj_zt = vzo * vot - vzt * voo
    adj_oo = vzz * vtt - vzt * vzt
    adj_ot = vzo * vzt - vzz * vot
    adj_tt = vzz * voo - vzo * vzo
    reciprocal = 1.0 / (vzz * adj_zz + vzo * adj_zo + vzt * adj_zt)
    inverse = [
        [entry_ * reciprocal for entry_ in line]
        for line in ((adj_zz, adj_zo, adj_zt), (adj_zo, adj_oo, adj_ot), (adj_zt, adj_ot, adj_tt))
    ]
    for residual in range(2):
        for obs in range(8):
            parts = [entry(obs, coordinate, residual) for coordinate in range(3)]
            for coordinate in range(3):
                if obs < 4:
                    value = (
                        parts[0] * inverse[0][coordinate]
                        + parts[1] * inverse[1][coordinate]
                        + parts[2] * inverse[2][coordinate]
                    )
                else:
                    value = parts[coordinate]
                row = (residual * 24 + obs * 3 + coordinate) * 16
                out_ref[row : row + 16, :] = value


def ranks(tile_ref, member_ref, rank_ref):
    for block in range(16):
        ids = jnp.broadcast_to(tile_ref[block : block + 1, :], (TILES, LANES))
        same = ids == lax.broadcasted_iota(jnp.int32, (TILES, LANES), 0)
        member_ref[block * TILES : (block + 1) * TILES, :] = jnp.where(same, 1.0, 0.0).astype(BF16)
    rows = lax.broadcasted_iota(jnp.int32, (LANES, LANES), 0)
    columns = lax.broadcasted_iota(jnp.int32, (LANES, LANES), 1)
    earlier = jnp.where(rows < columns, 1.0, 0.0).astype(BF16)
    members = member_ref[...]
    before = jnp.dot(members, earlier, preferred_element_type=F32)
    totals = jnp.dot(members, jnp.ones((LANES, LANES), BF16), preferred_element_type=F32)
    base = jnp.zeros((TILES, LANES), F32)
    for block in range(16):
        span = slice(block * TILES, (block + 1) * TILES)
        own = members[span].astype(F32) * (before[span] + base)
        rank_ref[block : block + 1, :] = jnp.sum(own, axis=0, keepdims=True)
        base = base + totals[span]


def gather_features(cam_ref, factor_ref, obs_ref, x_ref):
    for block in range(16):
        lanes = slice(block * LANES, (block + 1) * LANES)
        parts = [cam_ref[pl.ds(block * 2 + residual, 72, stride=32), :] for residual in range(2)]
        parts.append(factor_ref[pl.ds(block, 48, stride=16), :])
        values = jnp.concatenate(parts, axis=0)
        high = values.astype(BF16)
        x_ref[0:192, lanes] = high
        x_ref[208:400, lanes] = (values - high.astype(F32)).astype(BF16)
        names = obs_ref[:, lanes].astype(F32) + 1.0
        x_ref[192:208, lanes] = jnp.concatenate([names, jnp.zeros((8, LANES), F32)], axis=0).astype(BF16)


def place_points(x_ref, tile_ref, rank_ref, place_ref, wanted):
    slots = lax.broadcasted_iota(jnp.int32, (LANES, LANES), 0).astype(F32).astype(BF16)
    one, zero = jnp.ones((LANES, LANES), BF16), jnp.zeros((LANES, LANES), BF16)
    for part in range(2):
        slot_of = jnp.where(tile_ref[...] == wanted[part], rank_ref[...], -1.0)
        for block in range(16):
            row = jnp.broadcast_to(slot_of[block : block + 1, :], (LANES, LANES)).astype(BF16)
            place_ref[part * LANES : (part + 1) * LANES, block * LANES : (block + 1) * LANES] = jnp.where(
                row == slots, one, zero
            )
    placed = lax.dot_general(x_ref[...], place_ref[...], NT, preferred_element_type=F32)
    return placed[0:192] + placed[208:400], placed[192:200]


def fill_factor(block_ref, half, factor_ref, position):
    labels = (lax.broadcasted_iota(jnp.int32, (CAMB, LANES), 0).astype(F32) + 1.0).astype(BF16)
    cameras, masks, cross = [], [], []
    for index in range(4):
        obs = 4 * half + index
        camera = block_ref[CAM_ROW + obs : CAM_ROW + obs + 1, :]
        cameras.append(camera)
        masks.append(labels == jnp.broadcast_to(camera, (CAMB, LANES)).astype(BF16))
        camera_rows = [block_ref[res * 72 + obs * 9 : res * 72 + obs * 9 + 9, :] for res in range(2)]
        line = []
        for coordinate in range(3):
            rows = [PT_ROW + res * 24 + obs * 3 + coordinate for res in range(2)]
            line.append(
                camera_rows[0] * block_ref[rows[0] : rows[0] + 1, :]
                + camera_rows[1] * block_ref[rows[1] : rows[1] + 1, :]
            )
        cross.append(line)
    for index in range(4):
        for later in range(index + 1, 4):
            same = cameras[index] == cameras[later]
            for coordinate in range(3):
                cross[index][coordinate] = cross[index][coordinate] + jnp.where(same, cross[later][coordinate], 0.0)
    for coordinate in range(3):
        first = (coordinate * GROUP + position) * LANES
        for parameter in range(9):
            value = jnp.zeros((CAMB, LANES), BF16)
            for index in (3, 2, 1, 0):
                row = cross[index][coordinate][parameter : parameter + 1, :]
                value = jnp.where(masks[index], jnp.broadcast_to(row, (CAMB, LANES)).astype(BF16), value)
            factor_ref[parameter * CAMB : (parameter + 1) * CAMB, first : first + LANES] = value


def split_three(value):
    high = value.astype(BF16)
    rest = value - high.astype(F32)
    middle = rest.astype(BF16)
    return high, middle, (rest - middle.astype(F32)).astype(BF16)


def permute_columns(value, perm_ref):
    stacked = jnp.concatenate(split_three(value), axis=0)
    ordered = lax.dot_general(stacked, perm_ref[...], NT, preferred_element_type=F32)
    rows = value.shape[0]
    return ordered[0:rows] + ordered[rows : 2 * rows] + ordered[2 * rows :]


def kernel(
    cam_hbm, pt_hbm, obs_hbm, tile_hbm, upper_ref, lower_ref,
    cam_ref, pt_ref, obs_ref, tile_ref,
    x_ref, factor_ref, member_ref, rank_ref, place_ref, sent_ref, held_ref, relay_ref, left_ref, right_ref,
    total_ref, chain_a, chain_b, perm_ref, piece_ref, row_got, flip_ref, flip_got, lanes_ref,
    load_sem, sent_sem, held_sem, relay_sem, again_sem, chain_sent, chain_held, row_sent, row_held, flip_sent, flip_held,
):
    pt, row, col = lax.axis_index("pt"), lax.axis_index("row"), lax.axis_index("col")
    y, core = pt // 2, lax.rem(pt, 2)

    loads = [
        pltpu.make_async_copy(source, target, load_sem.at[index])
        for index, (source, target) in enumerate(
            ((tile_hbm, tile_ref), (pt_hbm, pt_ref), (obs_hbm, obs_ref), (cam_hbm, cam_ref))
        )
    ]
    for load in loads:
        load.start()

    def device(shift_y, shift_x, part):
        return (lax.rem(y + shift_y, 4) * 2 + (core if part == 0 else 1 - core), row, lax.rem(col + shift_x, 4))

    barrier = pltpu.get_barrier_semaphore()

    def greet(there):
        pl.semaphore_signal(barrier, inc=1, device_id=there, device_id_type=MESH)

    for part in range(2):
        for shift in range(1, 4):
            greet(device(0, shift, part))
            greet(device(shift, 0, part))
    greet(device(0, 0, 1))
    greet((pt, lax.rem(row + 1, 8), col))
    greet((pt, lax.rem(row + 7, 8), col))

    loads[0].wait()
    ranks(tile_ref, member_ref, rank_ref)
    loads[1].wait()
    point_factors(pt_ref, factor_ref)
    loads[2].wait()
    loads[3].wait()
    gather_features(cam_ref, factor_ref, obs_ref, x_ref)

    pl.semaphore_wait(barrier, 15)

    def single(index):
        far, along = index // 2 + 1, lax.rem(index, 2)
        return along * far, (1 - along) * far

    def double(index):
        return lax.rem(index + index // 3, 3) + 1, lax.rem(index, 3) + 1

    def direct(block, there):
        return pltpu.make_async_remote_copy(
            src_ref=sent_ref.at[block],
            dst_ref=held_ref.at[block],
            send_sem=sent_sem.at[block],
            recv_sem=held_sem.at[block],
            device_id=there,
            device_id_type=MESH,
        )

    def first_hop(block, there):
        return pltpu.make_async_remote_copy(
            src_ref=sent_ref.at[block],
            dst_ref=relay_ref.at[block - 2 * TWO_HOP],
            send_sem=sent_sem.at[block],
            recv_sem=relay_sem.at[block - 2 * TWO_HOP],
            device_id=there,
            device_id_type=MESH,
        )

    def second_hop(block, there):
        return pltpu.make_async_remote_copy(
            src_ref=relay_ref.at[block - 2 * TWO_HOP],
            dst_ref=held_ref.at[block],
            send_sem=again_sem.at[block - 2 * TWO_HOP],
            recv_sem=held_sem.at[block],
            device_id=there,
            device_id_type=MESH,
        )

    def place_pair(shift_y, shift_x):
        owners = [device(shift_y, shift_x, part) for part in range(2)]
        wanted = [owner[0] * 4 + owner[2] for owner in owners]
        placed, names = place_points(x_ref, tile_ref, rank_ref, place_ref, wanted)
        return owners, placed, names

    def store(target, block, placed, names, part):
        lanes = slice(part * LANES, (part + 1) * LANES)
        target[block, 0:192, :] = placed[:, lanes]
        target[block, 192:200, :] = names[:, lanes]

    def send_single(index, _):
        owners, placed, names = place_pair(*single(index))
        for part in range(2):
            block = 2 * (index + 1) + part
            store(sent_ref, block, placed, names, part)
            direct(block, owners[part]).start()
        return 0

    def send_double(index, _):
        shift_y, shift_x = double(index)
        _, placed, names = place_pair(shift_y, shift_x)
        block = 2 * (index + TWO_HOP)
        store(sent_ref, block, placed, names, 0)
        first_hop(block, device(0, shift_x, 0)).start()
        store(sent_ref, block + 1, placed, names, 1)
        first_hop(block + 1, device(shift_y, 0, 0)).start()
        return 0

    lax.fori_loop(0, 6, send_single, 0)
    lax.fori_loop(0, 9, send_double, 0)
    owners, placed, names = place_pair(0, 0)
    store(held_ref, 0, placed, names, 0)
    store(sent_ref, 1, placed, names, 1)
    direct(1, owners[1]).start()

    source = lax.broadcasted_iota(jnp.int32, (WIDTH, WIDTH), 1)
    goal = lax.broadcasted_iota(jnp.int32, (WIDTH, WIDTH), 0)
    perm_ref[...] = jnp.where((source & 63) * 9 + (source >> 6) == goal, 1.0, 0.0).astype(BF16)
    piece_ref[72:128, :] = jnp.zeros((56, WIDTH), F32)
    total_ref[...] = jnp.zeros_like(total_ref)

    def forward(index, _):
        shift_y, shift_x = double(index)
        block = 2 * (index + TWO_HOP)
        first_hop(block, (pt, row, col)).wait_recv()
        second_hop(block, device(shift_y, 0, 0)).start()
        first_hop(block + 1, (pt, row, col)).wait_recv()
        second_hop(block + 1, device(0, shift_x, 1)).start()
        return 0

    def add_group(group, _):
        start = jnp.where(group >= 5, 9, jnp.maximum(2 * group - 2, 0))
        stop = jnp.where(group >= 4, 9, 2 * group)
        lax.fori_loop(start, stop, forward, 0)
        for position in range(GROUP):
            index = group * GROUP + position

            @pl.when(index > 0)
            def _():
                direct(index, (pt, row, col)).wait_recv()

        for position in range(GROUP):
            block = held_ref.at[group * GROUP + position]
            fill_factor(block, 0, left_ref, position)
            fill_factor(block, 1, right_ref, position)
        product = lax.dot_general(left_ref[...], right_ref[...], NT, preferred_element_type=F32)
        total_ref[:, 0:64, :] -= product[0:512].reshape(8, 64, WIDTH)
        total_ref[:, 64:72, :] -= product[512:576].reshape(8, 8, WIDTH)
        return 0

    lax.fori_loop(0, TILES // GROUP, add_group, 0)

    ways = (jnp.where(core == 0, 1, 7), jnp.where(core == 0, 7, 1))
    chains = (chain_a, chain_b)
    hops = (4, 3)

    def piece_at(side, distance):
        return lax.rem(row + distance * ways[side], 8)

    def hop(side, step, chunk):
        span = slice(chunk * ROWS, (chunk + 1) * ROWS)
        source_ref = total_ref.at[piece_at(side, hops[side]), span] if step == 0 else chains[side].at[step - 1, span]
        return pltpu.make_async_remote_copy(
            src_ref=source_ref,
            dst_ref=chains[side].at[step, span],
            send_sem=chain_sent.at[side, step, chunk],
            recv_sem=chain_held.at[side, step, chunk],
            device_id=(pt, piece_at(side, 1), col),
            device_id_type=MESH,
        )

    there = lax.rem(pt + 4, 8)
    mirror = lax.rem(row + 4, 8)

    def send_row(other):
        return pltpu.make_async_remote_copy(
            src_ref=piece_ref.at[pl.ds(pl.multiple_of(other * 8, 8), 8), :],
            dst_ref=row_got.at[row],
            send_sem=row_sent.at[other],
            recv_sem=row_held.at[row],
            device_id=(other, pt, col),
            device_id_type=MESH,
        )

    def take_row(other):
        return pltpu.make_async_remote_copy(
            src_ref=piece_ref.at[pl.ds(pl.multiple_of(other * 8, 8), 8), :],
            dst_ref=row_got.at[other],
            send_sem=row_sent.at[other],
            recv_sem=row_held.at[other],
            device_id=(pt, row, col),
            device_id_type=MESH,
        )

    last_row = pltpu.make_async_remote_copy(
        src_ref=piece_ref.at[64:72, :],
        dst_ref=row_got.at[8],
        send_sem=row_sent.at[8],
        recv_sem=row_held.at[8],
        device_id=(row, pt, col),
        device_id_type=MESH,
    )

    def send_flip(other):
        return pltpu.make_async_remote_copy(
            src_ref=flip_ref.at[other],
            dst_ref=flip_got.at[row],
            send_sem=flip_sent.at[other],
            recv_sem=flip_held.at[row],
            device_id=(other, there, col),
            device_id_type=MESH,
        )

    def take_flip(other):
        return pltpu.make_async_remote_copy(
            src_ref=flip_ref.at[other],
            dst_ref=flip_got.at[other],
            send_sem=flip_sent.at[other],
            recv_sem=flip_held.at[other],
            device_id=(pt, row, col),
            device_id_type=MESH,
        )

    def start_row(other, _):
        is_self = (other == pt) & (pt == row)

        @pl.when(jnp.logical_not(is_self))
        def _():
            send_row(other).start()

        @pl.when(is_self)
        def _():
            row_got[row] = piece_ref[pl.ds(pl.multiple_of(other * 8, 8), 8), :]

        return 0

    def start_flip(index, _):
        other = lax.rem(pt + index, 8)
        is_self = (other == pt) & (there == row)

        @pl.when(jnp.logical_not(is_self))
        def _():
            send_flip(other).start()

        @pl.when(is_self)
        def _():
            flip_got[row] = flip_ref[other]

        return 0

    for chunk in range(CHUNKS):
        for side in range(2):
            hop(side, 0, chunk).start()
    for step in range(3):
        for chunk in range(CHUNKS):
            span = slice(chunk * ROWS, (chunk + 1) * ROWS)
            for side in range(2):
                if step < hops[side] - 1:
                    hop(side, step, chunk).wait_recv()
                    mine = total_ref[piece_at(side, hops[side] - 1 - step), span, :]
                    chains[side][step, span, :] = chains[side][step, span, :] + mine
                    hop(side, step + 1, chunk).start()
    for chunk in range(CHUNKS):
        span = slice(chunk * ROWS, (chunk + 1) * ROWS)
        hop(1, 2, chunk).wait_recv()
        hop(0, 3, chunk).wait_recv()
        piece_ref[span, :] = chain_a[3, span, :] + chain_b[2, span, :] + total_ref[row, span, :]
        lax.fori_loop(chunk * ROWS // 8, min((chunk + 1) * ROWS // 8, 8), start_row, 0)

    @pl.when(pt != row)
    def _():
        last_row.start()

    @pl.when(pt == row)
    def _():
        row_got[8] = piece_ref[64:72, :]

    flipped = piece_ref[...].T
    for other in range(8):
        for parameter in range(9):
            first = parameter * CAMB + other * 8
            flip_ref[other, parameter] = flipped[first : first + 8, :]
    lax.fori_loop(0, 8, start_flip, 0)

    def write_rows(target_ref, value):
        for parameter in range(9):
            for camera in range(8):
                goal_row, source_row = camera * 9 + parameter, parameter * 8 + camera
                target_ref[goal_row : goal_row + 1, :] = value[source_row : source_row + 1]

    for other in range(8):
        @pl.when((pt != row) | (row != other))
        def _():
            take_row(other).wait_recv()

    @pl.when(pt != row)
    def _():
        last_row.wait_recv()

    write_rows(upper_ref, permute_columns(row_got[...].reshape(72, WIDTH), perm_ref))

    for other in range(8):
        @pl.when((mirror != pt) | (row != other))
        def _():
            take_flip(other).wait_recv()

        block = flip_got[other].reshape(72, LANES)
        lanes_ref[:, other * 64 : (other + 1) * 64] = block[:, 0:64]
        lanes_ref[:, 512 + other * 8 : 520 + other * 8] = block[:, 64:72]
    write_rows(lower_ref, permute_columns(lanes_ref[...], perm_ref))

    def drain(block, _):
        direct(block, (pt, row, col)).wait_send()
        return 0

    def drain_again(block, _):
        second_hop(block, (pt, row, col)).wait_send()
        return 0

    lax.fori_loop(1, TILES, drain, 0)
    lax.fori_loop(2 * TWO_HOP, TILES, drain_again, 0)
    for side in range(2):
        for step in range(hops[side]):
            for chunk in range(CHUNKS):
                hop(side, step, chunk).wait_send()

    @pl.when(pt != row)
    def _():
        last_row.wait_send()

    def drain_blocks(other, _):
        @pl.when((other != pt) | (pt != row))
        def _():
            send_row(other).wait_send()

        @pl.when((other != pt) | (there != row))
        def _():
            send_flip(other).wait_send()

        return 0

    lax.fori_loop(0, 8, drain_blocks, 0)


def body(jac_cam, jac_pt, obs_cam, point_covisible_tile):
    def rows_of(array):
        observed, _, width, held = array.shape
        array = array.transpose(0, 2, 1, 3).reshape(observed * width, 2, held // LANES, LANES)
        return array.transpose(0, 2, 1, 3).reshape(observed * width * 2 * held // LANES, LANES)

    vmem = pl.BlockSpec(memory_space=pltpu.VMEM)
    upper, lower = pl.pallas_call(
        kernel,
        out_shape=[jax.ShapeDtypeStruct((72, WIDTH), F32)] * 2,
        in_specs=[pl.BlockSpec(memory_space=pl.ANY)] * 4,
        out_specs=[vmem] * 2,
        scratch_shapes=[
            pltpu.VMEM((2304, LANES), F32),
            pltpu.VMEM((768, LANES), F32),
            pltpu.VMEM((8, 2048), jnp.int32),
            pltpu.VMEM((16, LANES), jnp.int32),
            pltpu.VMEM((400, 2048), BF16),
            pltpu.VMEM((768, LANES), F32),
            pltpu.VMEM((512, LANES), BF16),
            pltpu.VMEM((16, LANES), F32),
            pltpu.VMEM((256, 2048), BF16),
            pltpu.VMEM((TILES, FEATURES, LANES), F32),
            pltpu.VMEM((TILES, FEATURES, LANES), F32),
            pltpu.VMEM((18, FEATURES, LANES), F32),
            pltpu.VMEM((WIDTH, 3 * LANES * GROUP), BF16),
            pltpu.VMEM((WIDTH, 3 * LANES * GROUP), BF16),
            pltpu.VMEM((8, 72, WIDTH), F32),
            pltpu.VMEM((4, 72, WIDTH), F32),
            pltpu.VMEM((3, 72, WIDTH), F32),
            pltpu.VMEM((WIDTH, WIDTH), BF16),
            pltpu.VMEM((LANES, WIDTH), F32),
            pltpu.VMEM((9, 8, WIDTH), F32),
            pltpu.VMEM((8, 9, 8, LANES), F32),
            pltpu.VMEM((8, 9, 8, LANES), F32),
            pltpu.VMEM((72, WIDTH), F32),
            pltpu.SemaphoreType.DMA((4,)),
            pltpu.SemaphoreType.DMA((TILES,)),
            pltpu.SemaphoreType.DMA((TILES,)),
            pltpu.SemaphoreType.DMA((18,)),
            pltpu.SemaphoreType.DMA((18,)),
            pltpu.SemaphoreType.DMA((2, 4, CHUNKS)),
            pltpu.SemaphoreType.DMA((2, 4, CHUNKS)),
            pltpu.SemaphoreType.DMA((9,)),
            pltpu.SemaphoreType.DMA((9,)),
            pltpu.SemaphoreType.DMA((8,)),
            pltpu.SemaphoreType.DMA((8,)),
        ],
        compiler_params=pltpu.CompilerParams(
            collective_id=0, has_side_effects=True, vmem_limit_bytes=50 * 2**20
        ),
    )(rows_of(jac_cam), rows_of(jac_pt), obs_cam, point_covisible_tile.reshape(16, LANES))
    return (upper[None], lower[None])


def solution(mesh):
    in_specs = (
        P(None, None, None, ("pt", "row", "col")),
        P(None, None, None, ("pt", "row", "col")),
        P(None, ("pt", "row", "col")),
        P(("pt", "row", "col"), None),
    )
    out_specs = (P(("row", "col"), "pt", None), P(("row", "col"), "pt", None))
    return jax.shard_map(body, mesh=mesh, in_specs=in_specs, out_specs=out_specs, check_vma=False)
```

time: 124 us -> 101 us (0.81); the launches traced: 121 us -> 100 us
  Pallas kernels: 116 us -> 94.7 us
    pallas_call x1, Pallas kernels: 116 us -> 94.7 us  [body(): pl.pallas_call(kernel, out_shape=[jax.ShapeDtypeStruct((72, WIDTH), F32)]...]
where the time goes in v2:
time: 101 us; the launch traced here: 100 us
  Pallas kernels  94.7 us (94%)
  local copies, waits for them, and re-layouts  5.14 us (5%)
    pallas_call x1, Pallas kernels, body(): pl.pallas_call(kernel, out_shape=[jax.ShapeDtypeStruct((72, WIDTH), F32)]...  94.7 us
    unnamed x10, local copies, waits for them, and re-layouts  5.14 us

profile of v2, /device:TPU:1, one launch (start us, length us, event | category | flops | bytes accessed | tf_op | source)
XLA Modules:
  0.0 100.5 jit_solution(1868932549650398491)
XLA Ops:
  0.6 0.0 copy-start
  0.6 1.3 %copy-done = f32[8,2,9,2048]{3,1,2,0:T(2,128)S(1)} copy-done((f32[8,2,9,2048]{3,1,2,0:T(2,128)S(1)}, f32[8,2,9,2048]{3,1,2,0:T(2,128)}, u32[]{:S(2)}) %copy-start) | copy-done | bytes 1179672
  1.9 0.0 copy-start.1
  1.9 1.0 copy-done.1
  2.9 0.0 copy-start.2
  2.9 0.8 copy-done.2
  3.7 0.0 copy-start.3
  3.7 0.7 copy-done.3
  4.4 94.7 %shard_map.59 = (f32[72,576]{1,0:T(8,128)S(1)}, f32[72,576]{1,0:T(8,128)S(1)}) custom-call(f32[2304,128]{1,0:T(8,128)S(1)} %bitcast.17, f32[768,128]{1,0:T(8,128)S(1)} %bitcast.18, s32[8,2048]{1,0:T(8,128)S(1)} %copy-done.2, s32[16,128]{1,0:T(8,128)S(1)} %bitcast.21), custom_call_target="tpu_custom_call" | custom-call | tf_op jit(solution)/shard_map/pallas_call | solution.py:517
  99.1 0.7 copy.10
  99.8 0.7 copy.11
Async XLA Ops:
  0.6 1.3 %copy-start = (f32[8,2,9,2048]{3,1,2,0:T(2,128)S(1)}, f32[8,2,9,2048]{3,1,2,0:T(2,128)}, u32[]{:S(2)}) copy-start(f32[8,2,9,2048]{3,1,2,0:T(2,128)} %param.4) | copy-start | bytes 3538948
  1.9 1.0 copy-start.1
  2.9 0.8 copy-start.2
  3.7 0.7 copy-start.3

commit v3 on v2

--- a/solution.py
+++ b/solution.py
@@ -18,7 +18,7 @@
 FEATURES = 200
 PT_ROW = 144
 CAM_ROW = 192
-GROUP = 4
+GROUP = 2
 WIDTH = 9 * CAMB
 NT = (((1,), (1,)), ((), ()))
 CHUNKS = 3
@@ -164,8 +164,8 @@
     cam_hbm, pt_hbm, obs_hbm, tile_hbm, upper_ref, lower_ref,
     cam_ref, pt_ref, obs_ref, tile_ref,
     x_ref, factor_ref, member_ref, rank_ref, place_ref, sent_ref, held_ref, relay_ref, left_ref, right_ref,
-    total_ref, chain_a, chain_b, perm_ref, piece_ref, row_got, flip_ref, flip_got, lanes_ref,
-    load_sem, sent_sem, held_sem, relay_sem, again_sem, chain_sent, chain_held, row_sent, row_held, flip_sent, flip_held,
+    total_ref, chain_a, chain_b, perm_ref, piece_ref, folded_ref, row_mid, row_got, flip_ref, flip_mid, flip_got, lanes_ref,
+    load_sem, sent_sem, held_sem, relay_sem, again_sem, chain_sent, chain_held, mid_sent, mid_held, end_sent, end_held, last_sem,
 ):
     pt, row, col = lax.axis_index("pt"), lax.axis_index("row"), lax.axis_index("col")
     y, core = pt // 2, lax.rem(pt, 2)
@@ -281,7 +281,7 @@
     source = lax.broadcasted_iota(jnp.int32, (WIDTH, WIDTH), 1)
     goal = lax.broadcasted_iota(jnp.int32, (WIDTH, WIDTH), 0)
     perm_ref[...] = jnp.where((source & 63) * 9 + (source >> 6) == goal, 1.0, 0.0).astype(BF16)
-    piece_ref[72:128, :] = jnp.zeros((56, WIDTH), F32)
+    folded_ref[...] = jnp.zeros_like(folded_ref)
     total_ref[...] = jnp.zeros_like(total_ref)
 
     def forward(index, _):
@@ -294,8 +294,8 @@
         return 0
 
     def add_group(group, _):
-        start = jnp.where(group >= 5, 9, jnp.maximum(2 * group - 2, 0))
-        stop = jnp.where(group >= 4, 9, 2 * group)
+        start = jnp.where(group >= 9, 9, jnp.maximum(group - 1, 0))
+        stop = jnp.where(group >= 8, 9, group)
         lax.fori_loop(start, stop, forward, 0)
         for position in range(GROUP):
             index = group * GROUP + position
@@ -334,84 +334,79 @@
             device_id_type=MESH,
         )
 
-    there = lax.rem(pt + 4, 8)
     mirror = lax.rem(row + 4, 8)
-
-    def send_row(other):
+    middles = (row_mid, flip_mid)
+    ends = (row_got, flip_got)
+
+    def block_of(kind, other):
+        if kind == 1:
+            return flip_ref.at[other]
+        return piece_ref.at[pl.ds(pl.multiple_of(other * 8, 8), 8), :]
+
+    def to_middle(kind, other, slot):
         return pltpu.make_async_remote_copy(
-            src_ref=piece_ref.at[pl.ds(pl.multiple_of(other * 8, 8), 8), :],
-            dst_ref=row_got.at[row],
-            send_sem=row_sent.at[other],
-            recv_sem=row_held.at[row],
-            device_id=(other, pt, col),
+            src_ref=block_of(kind, other),
+            dst_ref=middles[kind].at[slot],
+            send_sem=mid_sent.at[kind, other],
+            recv_sem=mid_held.at[kind, slot],
+            device_id=(other, row, col),
             device_id_type=MESH,
         )
 
-    def take_row(other):
+    def to_end(kind, other, slot):
         return pltpu.make_async_remote_copy(
-            src_ref=piece_ref.at[pl.ds(pl.multiple_of(other * 8, 8), 8), :],
-            dst_ref=row_got.at[other],
-            send_sem=row_sent.at[other],
-            recv_sem=row_held.at[other],
-            device_id=(pt, row, col),
+            src_ref=middles[kind].at[other],
+            dst_ref=ends[kind].at[slot],
+            send_sem=end_sent.at[kind, other],
+            recv_sem=end_held.at[kind, slot],
+            device_id=(pt, other if kind == 0 else lax.rem(other + 4, 8), col),
             device_id_type=MESH,
         )
 
     last_row = pltpu.make_async_remote_copy(
         src_ref=piece_ref.at[64:72, :],
         dst_ref=row_got.at[8],
-        send_sem=row_sent.at[8],
-        recv_sem=row_held.at[8],
+        send_sem=last_sem.at[0],
+        recv_sem=last_sem.at[1],
         device_id=(row, pt, col),
         device_id_type=MESH,
     )
 
-    def send_flip(other):
-        return pltpu.make_async_remote_copy(
-            src_ref=flip_ref.at[other],
-            dst_ref=flip_got.at[row],
-            send_sem=flip_sent.at[other],
-            recv_sem=flip_held.at[row],
-            device_id=(other, there, col),
-            device_id_type=MESH,
-        )
-
-    def take_flip(other):
-        return pltpu.make_async_remote_copy(
-            src_ref=flip_ref.at[other],
-            dst_ref=flip_got.at[other],
-            send_sem=flip_sent.at[other],
-            recv_sem=flip_held.at[other],
-            device_id=(pt, row, col),
-            device_id_type=MESH,
-        )
-
-    def start_row(other, _):
-        is_self = (other == pt) & (pt == row)
-
-        @pl.when(jnp.logical_not(is_self))
-        def _():
-            send_row(other).start()
-
-        @pl.when(is_self)
-        def _():
-            row_got[row] = piece_ref[pl.ds(pl.multiple_of(other * 8, 8), 8), :]
-
-        return 0
-
-    def start_flip(index, _):
-        other = lax.rem(pt + index, 8)
-        is_self = (other == pt) & (there == row)
-
-        @pl.when(jnp.logical_not(is_self))
-        def _():
-            send_flip(other).start()
-
-        @pl.when(is_self)
-        def _():
-            flip_got[row] = flip_ref[other]
-
-        return 0
+    def start_middle(kind, first, last):
+        def start(other, _):
+            @pl.when(other != pt)
+            def _():
+                to_middle(kind, other, pt).start()
+
+            @pl.when(other == pt)
+            def _():
+                middles[kind][other] = block_of(kind, other)[...]
+
+            return 0
+
+        lax.fori_loop(first, last, start, 0)
+
+    def start_end(kind):
+        own = row if kind == 0 else mirror
+
+        def start(index, _):
+            other = lax.rem(pt + index, 8)
+
+            @pl.when(other != pt)
+            def _():
+                to_middle(kind, other, other).wait_recv()
+
+            @pl.when(other != own)
+            def _():
+                to_end(kind, other, row).start()
+
+            @pl.when(other == own)
+            def _():
+                ends[kind][row] = middles[kind][other]
+
+            return 0
+
+        lax.fori_loop(0, 8, start, 0)
 
     for chunk in range(CHUNKS):
         for side in range(2):
@@ -430,7 +425,7 @@
         hop(1, 2, chunk).wait_recv()
         hop(0, 3, chunk).wait_recv()
         piece_ref[span, :] = chain_a[3, span, :] + chain_b[2, span, :] + total_ref[row, span, :]
-        lax.fori_loop(chunk * ROWS // 8, min((chunk + 1) * ROWS // 8, 8), start_row, 0)
+        start_middle(0, chunk * ROWS // 8, min((chunk + 1) * ROWS // 8, 8))
 
     @pl.when(pt != row)
     def _():
@@ -440,12 +435,22 @@
     def _():
         row_got[8] = piece_ref[64:72, :]
 
-    flipped = piece_ref[...].T
+    folded_ref[0:64, 0:256] = piece_ref[0:64, 0:256]
+    folded_ref[64:128, 0:256] = piece_ref[0:64, 256:512]
+    folded_ref[0:64, 256:320] = piece_ref[0:64, 512:576]
+    for parameter in range(8):
+        folded_ref[64 + parameter * 8 : 72 + parameter * 8, 256:320] = piece_ref[
+            64:72, parameter * 64 : (parameter + 1) * 64
+        ]
+    folded_ref[0:8, 320:384] = piece_ref[64:72, 512:576]
+    flipped = folded_ref[...].T
     for other in range(8):
-        for parameter in range(9):
-            first = parameter * CAMB + other * 8
-            flip_ref[other, parameter] = flipped[first : first + 8, :]
-    lax.fori_loop(0, 8, start_flip, 0)
+        for tile in range(6):
+            first = tile * CAMB + other * 8
+            flip_ref[other, tile] = flipped[first : first + 8, :]
+    start_middle(1, 0, 8)
+    start_end(0)
+    start_end(1)
 
     def write_rows(target_ref, value):
         for parameter in range(9):
@@ -454,9 +459,9 @@
                 target_ref[goal_row : goal_row + 1, :] = value[source_row : source_row + 1]
 
     for other in range(8):
-        @pl.when((pt != row) | (row != other))
+        @pl.when(row != other)
         def _():
-            take_row(other).wait_recv()
+            to_end(0, other, other).wait_recv()
 
     @pl.when(pt != row)
     def _():
@@ -465,13 +470,16 @@
     write_rows(upper_ref, permute_columns(row_got[...].reshape(72, WIDTH), perm_ref))
 
     for other in range(8):
-        @pl.when((mirror != pt) | (row != other))
+        @pl.when(row != other)
         def _():
-            take_flip(other).wait_recv()
-
-        block = flip_got[other].reshape(72, LANES)
-        lanes_ref[:, other * 64 : (other + 1) * 64] = block[:, 0:64]
-        lanes_ref[:, 512 + other * 8 : 520 + other * 8] = block[:, 64:72]
+            to_end(1, other, other).wait_recv()
+
+        for parameter in range(9):
+            rows = slice(parameter * 8, (parameter + 1) * 8)
+            tile, lane = (4, 0) if parameter == 8 else (parameter % 4, parameter // 4 * 64)
+            lanes_ref[rows, other * 64 : (other + 1) * 64] = flip_got[other, tile, :, lane : lane + 64]
+            tile, lane = (5, 0) if parameter == 8 else (4, 64 + parameter * 8)
+            lanes_ref[rows, 512 + other * 8 : 520 + other * 8] = flip_got[other, tile, :, lane : lane + 8]
     write_rows(lower_ref, permute_columns(lanes_ref[...], perm_ref))
 
     def drain(block, _):
@@ -494,13 +502,15 @@
         last_row.wait_send()
 
     def drain_blocks(other, _):
-        @pl.when((other != pt) | (pt != row))
-        def _():
-            send_row(other).wait_send()
-
-        @pl.when((other != pt) | (there != row))
-        def _():
-            send_flip(other).wait_send()
+        for kind in range(2):
+
+            @pl.when(other != pt)
+            def _(kind=kind):
+                to_middle(kind, other, pt).wait_send()
+
+            @pl.when(other != (row if kind == 0 else mirror))
+            def _(kind=kind):
+                to_end(kind, other, row).wait_send()
 
         return 0
 
@@ -538,10 +548,13 @@
             pltpu.VMEM((4, 72, WIDTH), F32),
             pltpu.VMEM((3, 72, WIDTH), F32),
             pltpu.VMEM((WIDTH, WIDTH), BF16),
-            pltpu.VMEM((LANES, WIDTH), F32),
+            pltpu.VMEM((72, WIDTH), F32),
+            pltpu.VMEM((LANES, 384), F32),
+            pltpu.VMEM((8, 8, WIDTH), F32),
             pltpu.VMEM((9, 8, WIDTH), F32),
-            pltpu.VMEM((8, 9, 8, LANES), F32),
-            pltpu.VMEM((8, 9, 8, LANES), F32),
+            pltpu.VMEM((8, 6, 8, LANES), F32),
+            pltpu.VMEM((8, 6, 8, LANES), F32),
+            pltpu.VMEM((8, 6, 8, LANES), F32),
             pltpu.VMEM((72, WIDTH), F32),
             pltpu.SemaphoreType.DMA((4,)),
             pltpu.SemaphoreType.DMA((TILES,)),
@@ -550,13 +563,14 @@
             pltpu.SemaphoreType.DMA((18,)),
             pltpu.SemaphoreType.DMA((2, 4, CHUNKS)),
             pltpu.SemaphoreType.DMA((2, 4, CHUNKS)),
-            pltpu.SemaphoreType.DMA((9,)),
-            pltpu.SemaphoreType.DMA((9,)),
-            pltpu.SemaphoreType.DMA((8,)),
-            pltpu.SemaphoreType.DMA((8,)),
+            pltpu.SemaphoreType.DMA((2, 8)),
+            pltpu.SemaphoreType.DMA((2, 8)),
+            pltpu.SemaphoreType.DMA((2, 8)),
+            pltpu.SemaphoreType.DMA((2, 8)),
+            pltpu.SemaphoreType.DMA((2,)),
         ],
         compiler_params=pltpu.CompilerParams(
-            collective_id=0, has_side_effects=True, vmem_limit_bytes=50 * 2**20
+            collective_id=0, has_side_effects=True, vmem_limit_bytes=64 * 2**20 - 2**19
         ),
     )(rows_of(jac_cam), rows_of(jac_pt), obs_cam, point_covisible_tile.reshape(16, LANES))
     return (upper[None], lower[None])

time: 101 us -> 91.2 us (0.903)
  Pallas kernels: 94.7 us -> 87.2 us
  local copies, waits for them, and re-layouts: 5.14 us -> 3.22 us
    pallas_call x1, Pallas kernels: 94.7 us -> 87.2 us  [body(): pl.pallas_call(kernel, out_shape=[jax.ShapeDtypeStruct((72, WIDTH), F32)]...]
    unnamed x10 -> x2, local copies, waits for them, and re-layouts: 5.14 us -> 3.22 us
where the time goes in v3:
time: 91.2 us; the launch traced here: 91.1 us
  Pallas kernels  87.2 us (96%)
  local copies, waits for them, and re-layouts  3.22 us (4%)
    pallas_call x1, Pallas kernels, body(): pl.pallas_call(kernel, out_shape=[jax.ShapeDtypeStruct((72, WIDTH), F32)]...  87.2 us
    unnamed x2, local copies, waits for them, and re-layouts  3.22 us

profile of v3, /device:TPU:1, one launch (start us, length us, event | category | flops | bytes accessed | tf_op | source)
XLA Modules:
  0.0 91.1 jit_solution(11213522064904968783)
XLA Ops:
  0.6 87.2 %shard_map.59 = (f32[72,576]{1,0:T(8,128)}, f32[72,576]{1,0:T(8,128)}) custom-call(f32[2304,128]{1,0:T(8,128)} %bitcast.17, f32[768,128]{1,0:T(8,128)} %bitcast.18, s32[8,2048]{1,0:T(8,128)} %obs_hbm.1, s32[16,128]{1,0:T(8,128)} %bitcast.21), custom_call_target="tpu_custom_call" | custom-call | tf_op jit(solution)/shard_map/pallas_call | solution.py:527
  87.9 1.6 %copy.10 = f32[1,72,576]{2,1,0:T(8,128)} copy(f32[1,72,576]{2,1,0:T(8,128)} %bitcast.20) | data formatting | bytes 331776
  89.5 1.6 %copy.11 = f32[1,72,576]{2,1,0:T(8,128)} copy(f32[1,72,576]{2,1,0:T(8,128)} %bitcast.19) | data formatting | bytes 331776

commit v4 on v3

--- a/solution.py
+++ b/solution.py
@@ -164,7 +164,7 @@
     cam_hbm, pt_hbm, obs_hbm, tile_hbm, upper_ref, lower_ref,
     cam_ref, pt_ref, obs_ref, tile_ref,
     x_ref, factor_ref, member_ref, rank_ref, place_ref, sent_ref, held_ref, relay_ref, left_ref, right_ref,
-    total_ref, chain_a, chain_b, perm_ref, piece_ref, folded_ref, row_mid, row_got, flip_ref, flip_mid, flip_got, lanes_ref,
+    total_ref, chain_a, chain_b, piece_ref, folded_ref, row_mid, row_got, flip_ref, flip_mid, flip_got, lanes_ref,
     load_sem, sent_sem, held_sem, relay_sem, again_sem, chain_sent, chain_held, mid_sent, mid_held, end_sent, end_held, last_sem,
 ):
     pt, row, col = lax.axis_index("pt"), lax.axis_index("row"), lax.axis_index("col")
@@ -271,19 +271,6 @@
         first_hop(block + 1, device(shift_y, 0, 0)).start()
         return 0
 
-    lax.fori_loop(0, 6, send_single, 0)
-    lax.fori_loop(0, 9, send_double, 0)
-    owners, placed, names = place_pair(0, 0)
-    store(held_ref, 0, placed, names, 0)
-    store(sent_ref, 1, placed, names, 1)
-    direct(1, owners[1]).start()
-
-    source = lax.broadcasted_iota(jnp.int32, (WIDTH, WIDTH), 1)
-    goal = lax.broadcasted_iota(jnp.int32, (WIDTH, WIDTH), 0)
-    perm_ref[...] = jnp.where((source & 63) * 9 + (source >> 6) == goal, 1.0, 0.0).astype(BF16)
-    folded_ref[...] = jnp.zeros_like(folded_ref)
-    total_ref[...] = jnp.zeros_like(total_ref)
-
     def forward(index, _):
         shift_y, shift_x = double(index)
         block = 2 * (index + TWO_HOP)
@@ -293,9 +280,20 @@
         second_hop(block + 1, device(0, shift_x, 1)).start()
         return 0
 
+    lax.fori_loop(0, 9, send_double, 0)
+    lax.fori_loop(0, 6, send_single, 0)
+    lax.fori_loop(0, 3, forward, 0)
+    owners, placed, names = place_pair(0, 0)
+    store(held_ref, 0, placed, names, 0)
+    store(sent_ref, 1, placed, names, 1)
+    direct(1, owners[1]).start()
+
+    folded_ref[...] = jnp.zeros_like(folded_ref)
+    total_ref[...] = jnp.zeros_like(total_ref)
+
     def add_group(group, _):
-        start = jnp.where(group >= 9, 9, jnp.maximum(group - 1, 0))
-        stop = jnp.where(group >= 8, 9, group)
+        start = jnp.minimum(2 * group + 3, 9)
+        stop = jnp.minimum(2 * group + 5, 9)
         lax.fori_loop(start, stop, forward, 0)
         for position in range(GROUP):
             index = group * GROUP + position
@@ -452,12 +450,6 @@
     start_end(0)
     start_end(1)
 
-    def write_rows(target_ref, value):
-        for parameter in range(9):
-            for camera in range(8):
-                goal_row, source_row = camera * 9 + parameter, parameter * 8 + camera
-                target_ref[goal_row : goal_row + 1, :] = value[source_row : source_row + 1]
-
     for other in range(8):
         @pl.when(row != other)
         def _():
@@ -467,7 +459,7 @@
     def _():
         last_row.wait_recv()
 
-    write_rows(upper_ref, permute_columns(row_got[...].reshape(72, WIDTH), perm_ref))
+    upper_ref[...] = row_got[...].reshape(72, WIDTH)
 
     for other in range(8):
         @pl.when(row != other)
@@ -480,7 +472,7 @@
             lanes_ref[rows, other * 64 : (other + 1) * 64] = flip_got[other, tile, :, lane : lane + 64]
             tile, lane = (5, 0) if parameter == 8 else (4, 64 + parameter * 8)
             lanes_ref[rows, 512 + other * 8 : 520 + other * 8] = flip_got[other, tile, :, lane : lane + 8]
-    write_rows(lower_ref, permute_columns(lanes_ref[...], perm_ref))
+    lower_ref[...] = lanes_ref[...]
 
     def drain(block, _):
         direct(block, (pt, row, col)).wait_send()
@@ -515,6 +507,21 @@
         return 0
 
     lax.fori_loop(0, 8, drain_blocks, 0)
+
+
+def order(upper_in, lower_in, upper_ref, lower_ref, perm_ref):
+    source = lax.broadcasted_iota(jnp.int32, (WIDTH, WIDTH), 1)
+    goal = lax.broadcasted_iota(jnp.int32, (WIDTH, WIDTH), 0)
+    perm_ref[...] = jnp.where((source & 63) * 9 + (source >> 6) == goal, 1.0, 0.0).astype(BF16)
+
+    def write_rows(target_ref, value):
+        for parameter in range(9):
+            for camera in range(8):
+                goal_row, source_row = camera * 9 + parameter, parameter * 8 + camera
+                target_ref[goal_row : goal_row + 1, :] = value[source_row : source_row + 1]
+
+    write_rows(upper_ref, permute_columns(upper_in[...], perm_ref))
+    write_rows(lower_ref, permute_columns(lower_in[...], perm_ref))
 
 
 def body(jac_cam, jac_pt, obs_cam, point_covisible_tile):
@@ -547,7 +554,6 @@
             pltpu.VMEM((8, 72, WIDTH), F32),
             pltpu.VMEM((4, 72, WIDTH), F32),
             pltpu.VMEM((3, 72, WIDTH), F32),
-            pltpu.VMEM((WIDTH, WIDTH), BF16),
             pltpu.VMEM((72, WIDTH), F32),
             pltpu.VMEM((LANES, 384), F32),
             pltpu.VMEM((8, 8, WIDTH), F32),
@@ -573,6 +579,14 @@
             collective_id=0, has_side_effects=True, vmem_limit_bytes=64 * 2**20 - 2**19
         ),
     )(rows_of(jac_cam), rows_of(jac_pt), obs_cam, point_covisible_tile.reshape(16, LANES))
+    upper, lower = pl.pallas_call(
+        order,
+        out_shape=[jax.ShapeDtypeStruct((72, WIDTH), F32)] * 2,
+        in_specs=[vmem] * 2,
+        out_specs=[vmem] * 2,
+        scratch_shapes=[pltpu.VMEM((WIDTH, WIDTH), BF16)],
+        compiler_params=pltpu.CompilerParams(vmem_limit_bytes=64 * 2**20 - 2**19),
+    )(upper, lower)
     return (upper[None], lower[None])
 
 

time: 91.2 us -> 89.6 us (0.982)
  local copies, waits for them, and re-layouts: 3.22 us -> 0 us
  Pallas kernels: 87.2 us -> 88.8 us
    unnamed x2 -> x0, local copies, waits for them, and re-layouts: 3.22 us -> none
    pallas_call x0 -> x1, Pallas kernels: none -> 2.58 us  [body(): pl.pallas_call(order, out_shape=[jax.ShapeDtypeStruct((72, WIDTH), F32)]...]
    pallas_call x1, Pallas kernels: 87.2 us -> 86.2 us  [body(): pl.pallas_call(kernel, out_shape=[jax.ShapeDtypeStruct((72, WIDTH), F32)]...]
where the time goes in v4:
time: 89.6 us; the launch traced here: 89.4 us
  Pallas kernels  88.8 us (99%)
    pallas_call x1, Pallas kernels, body(): pl.pallas_call(kernel, out_shape=[jax.ShapeDtypeStruct((72, WIDTH), F32)]...  86.2 us
    pallas_call x1, Pallas kernels, body(): pl.pallas_call(order, out_shape=[jax.ShapeDtypeStruct((72, WIDTH), F32)]...  2.58 us

profile of v4, /device:TPU:1, one launch (start us, length us, event | category | flops | bytes accessed | tf_op | source)
XLA Modules:
  0.0 89.4 jit_solution(11920449870725587140)
XLA Ops:
  0.6 86.2 %shard_map.59 = (f32[72,576]{1,0:T(8,128)}, f32[72,576]{1,0:T(8,128)}) custom-call(f32[2304,128]{1,0:T(8,128)} %bitcast.17, f32[768,128]{1,0:T(8,128)} %bitcast.18, s32[8,2048]{1,0:T(8,128)} %obs_hbm.1, s32[16,128]{1,0:T(8,128)} %bitcast.19), custom_call_target="tpu_custom_call" | custom-call | tf_op jit(solution)/shard_map/pallas_call | solution.py:534
  86.9 2.6 %shard_map.60 = (f32[72,576]{1,0:T(8,128)}, f32[72,576]{1,0:T(8,128)}) custom-call(f32[72,576]{1,0:T(8,128)} %get-tuple-element.6.upper_in, f32[72,576]{1,0:T(8,128)} %get-tuple-element.7.lower_in), custom_call_target="tpu_custom_call" | custom-call | tf_op jit(solution)/shard_map/pallas_call | solution.py:582

commit v5 on v4

--- a/solution.py
+++ b/solution.py
@@ -409,6 +409,18 @@
     for chunk in range(CHUNKS):
         for side in range(2):
             hop(side, 0, chunk).start()
+
+    def drain(block, _):
+        direct(block, (pt, row, col)).wait_send()
+        return 0
+
+    def drain_again(block, _):
+        second_hop(block, (pt, row, col)).wait_send()
+        return 0
+
+    lax.fori_loop(1, TILES, drain, 0)
+    lax.fori_loop(2 * TWO_HOP, TILES, drain_again, 0)
+
     for step in range(3):
         for chunk in range(CHUNKS):
             span = slice(chunk * ROWS, (chunk + 1) * ROWS)
@@ -449,6 +461,10 @@
     start_middle(1, 0, 8)
     start_end(0)
     start_end(1)
+    for side in range(2):
+        for step in range(hops[side]):
+            for chunk in range(CHUNKS):
+                hop(side, step, chunk).wait_send()
 
     for other in range(8):
         @pl.when(row != other)
@@ -474,20 +490,6 @@
             lanes_ref[rows, 512 + other * 8 : 520 + other * 8] = flip_got[other, tile, :, lane : lane + 8]
     lower_ref[...] = lanes_ref[...]
 
-    def drain(block, _):
-        direct(block, (pt, row, col)).wait_send()
-        return 0
-
-    def drain_again(block, _):
-        second_hop(block, (pt, row, col)).wait_send()
-        return 0
-
-    lax.fori_loop(1, TILES, drain, 0)
-    lax.fori_loop(2 * TWO_HOP, TILES, drain_again, 0)
-    for side in range(2):
-        for step in range(hops[side]):
-            for chunk in range(CHUNKS):
-                hop(side, step, chunk).wait_send()
 
     @pl.when(pt != row)
     def _():

time: 89.6 us -> 89.2 us (level)
  no operation moved by 1% of the time
where the time goes in v5:
time: 89.2 us; the launch traced here: 89.1 us
  Pallas kernels  88.4 us (99%)
    pallas_call x1, Pallas kernels, body(): pl.pallas_call(kernel, out_shape=[jax.ShapeDtypeStruct((72, WIDTH), F32)]...  85.9 us
    pallas_call x1, Pallas kernels, body(): pl.pallas_call(order, out_shape=[jax.ShapeDtypeStruct((72, WIDTH), F32)]...  2.58 us

profile of v5, /device:TPU:1, one launch (start us, length us, event | category | flops | bytes accessed | tf_op | source)
XLA Modules:
  0.0 89.1 jit_solution(18305421232689569318)
XLA Ops:
  0.6 85.9 %shard_map.59 = (f32[72,576]{1,0:T(8,128)}, f32[72,576]{1,0:T(8,128)}) custom-call(f32[2304,128]{1,0:T(8,128)} %bitcast.17, f32[768,128]{1,0:T(8,128)} %bitcast.18, s32[8,2048]{1,0:T(8,128)} %obs_hbm.1, s32[16,128]{1,0:T(8,128)} %bitcast.19), custom_call_target="tpu_custom_call" | custom-call | tf_op jit(solution)/shard_map/pallas_call | solution.py:536
  86.5 2.6 %shard_map.60 = (f32[72,576]{1,0:T(8,128)}, f32[72,576]{1,0:T(8,128)}) custom-call(f32[72,576]{1,0:T(8,128)} %get-tuple-element.6.upper_in, f32[72,576]{1,0:T(8,128)} %get-tuple-element.7.lower_in), custom_call_target="tpu_custom_call" | custom-call | tf_op jit(solution)/shard_map/pallas_call | solution.py:584
